TPU v7x, 512 devices: a whole 4x8x8 slice. The times are simulated.
512 devices in a mesh: row: 16 (over x, z_lo, core), col: 4 (over z_hi), depth: 8 (over y).
Axes of the slice: x: 4, y: 8, z: 8 (z_hi: 4, z_lo: 2; z = z_hi * 2 + z_lo), core: 2. Of those that a mesh axis runs over, the one named last changes fastest.
Arguments:
- normed: bfloat16 [4096, 3072], P(('depth', 'row'), 'col'), may hold values from -6 to 6
- up_weight: bfloat16 [3072, 12288], P('col', 'row'), may hold values from -0.109375 to 0.109375
- down_weight: bfloat16 [12288, 3072], P('row', 'col'), may hold values from -0.0546875 to 0.0546875
- out_grad: bfloat16 [4096, 3072], P(('depth', 'row'), 'col'), may hold values from -6 to 6
Outputs:
- branch_out: bfloat16 [4096, 3072], P(('depth', 'row'), 'col')
- normed_grad: bfloat16 [4096, 3072], P(('depth', 'row'), 'col')
- up_grad: float32 [3072, 12288], P(('col', 'depth'), 'row')
- down_grad: float32 [12288, 3072], P(('row', 'depth'), 'col')
All inputs are finite; a program needn't handle non-finite values.
Results may differ from a plain program's by a relative error of at most 0.029.
Values may be sent and summed in bfloat16 or wider, within the bound.
A program may use at most 64 MiB of HBM per device.

v0:
```python
import math

import jax
import jax.numpy as jnp
from jax import lax
from jax.sharding import PartitionSpec as P


def gelu_parts(value):
    coeff = math.sqrt(2.0 / math.pi)
    inner = coeff * (value + 0.044715 * value * value * value)
    tangent = jnp.tanh(inner)
    activated = 0.5 * value * (1.0 + tangent)
    slope = 0.5 * (1.0 + tangent) + 0.5 * value * (1.0 - tangent * tangent) * coeff * (
        1.0 + 3.0 * 0.044715 * value * value
    )
    return (activated, slope)


def contract_last(left, right):
    return lax.dot_general(
        left, right, (((1,), (1,)), ((), ())), preferred_element_type=jnp.float32
    )


def contract_first(left, right):
    return lax.dot_general(
        left, right, (((0,), (0,)), ((), ())), preferred_element_type=jnp.float32
    )


def per_device(normed, up_weight, down_weight, out_grad):
    gathered, cotangent = (
        lax.all_gather(normed, "row", axis=0, tiled=True),
        lax.all_gather(out_grad, "row", axis=0, tiled=True),
    )
    up_part = jnp.dot(gathered, up_weight, preferred_element_type=jnp.float32)
    back_part = contract_last(cotangent, down_weight)
    pre_act, back_act = (
        lax.psum(up_part.astype(jnp.bfloat16), "col").astype(jnp.float32),
        lax.psum(back_part.astype(jnp.bfloat16), "col").astype(jnp.float32),
    )
    active_full, slope = gelu_parts(pre_act)
    activated = active_full.astype(jnp.bfloat16)
    pre_grad = (back_act * slope).astype(jnp.bfloat16)
    out_part = jnp.dot(activated, down_weight, preferred_element_type=jnp.float32)
    input_part = contract_last(pre_grad, up_weight)
    branch_sum, input_sum = (
        lax.psum_scatter(
            out_part.astype(jnp.bfloat16), "row", scatter_dimension=0, tiled=True
        ).astype(jnp.float32),
        lax.psum_scatter(
            input_part.astype(jnp.bfloat16), "row", scatter_dimension=0, tiled=True
        ).astype(jnp.float32),
    )
    up_local = contract_first(gathered, pre_grad)
    down_local = contract_first(activated, cotangent)
    up_total, down_total = (
        lax.psum(up_local.astype(jnp.bfloat16), "depth").astype(jnp.float32),
        lax.psum(down_local.astype(jnp.bfloat16), "depth").astype(jnp.float32),
    )
    layers = lax.axis_size("depth")
    depth_index = lax.axis_index("depth")
    up_rows = up_local.shape[0] // layers
    down_rows = down_local.shape[0] // layers
    up_sum = lax.dynamic_slice_in_dim(up_total, depth_index * up_rows, up_rows, 0)
    down_sum = lax.dynamic_slice_in_dim(down_total, depth_index * down_rows, down_rows, 0)
    factor = 1.0 / math.sqrt(gathered.shape[0] * lax.axis_size("depth"))
    return (
        branch_sum.astype(jnp.bfloat16),
        input_sum.astype(jnp.bfloat16),
        up_sum * factor,
        down_sum * factor,
    )


def solution(mesh):
    return jax.shard_map(
        per_device,
        mesh=mesh,
        in_specs=(
            P(("depth", "row"), "col"),
            P("col", "row"),
            P("row", "col"),
            P(("depth", "row"), "col"),
        ),
        out_specs=(
            P(("depth", "row"), "col"),
            P(("depth", "row"), "col"),
            P(("col", "depth"), "row"),
            P(("row", "depth"), "col"),
        ),
        check_vma=False,
    )
```

profile of v0, /device:TPU:1, one launch (start us, length us, event | category | flops | bytes accessed | tf_op | source)
XLA Modules:
  0.0 381.2 jit_solution(2808030847214560351)
XLA Ops:
  7.2 0.0 copy-start
  7.2 0.0 all-reduce.7.cloned.1.call-start
  7.2 27.8 %all_gather.6 = bf16[512,768]{1,0:T(8,128)(2,1)S(1)} all-gather(bf16[32,768]{1,0:T(8,128)(2,1)} %param.4), channel_id=1, replica_groups=mesh['row'=16,'col'=4,'depth'=8] {'row'}, dimensions={0}, use_global_device_ids=true | all-gather | bytes 835584 | tf_op jit(solution)/shard_map/all_gather | solution.py:34
  35.1 20.3 %all_gather.7 = bf16[512,768]{1,0:T(8,128)(2,1)S(1)} all-gather(bf16[32,768]{1,0:T(8,128)(2,1)} %param.7), channel_id=1, replica_groups=mesh['row'=16,'col'=4,'depth'=8] {'row'}, dimensions={0}, use_global_device_ids=true | all-gather | bytes 835584 | tf_op jit(solution)/shard_map/all_gather | solution.py:35
  55.4 1.7 convolution_convert_fusion.5
  57.0 1.7 convolution_convert_fusion.3
  58.8 0.0 all-reduce.7.cloned.1.call-update
  58.8 0.0 all-reduce.5.cloned.1.call-start
  58.8 88.3 %all-reduce.7.cloned.1.call-done = (bf16[512,768]{1,0:T(8,128)(2,1)}, bf16[512,768]{1,0:T(8,128)(2,1)}) async-done(((bf16[512,768]{1,0:T(8,128)(2,1)}, bf16[512,768]{1,0:T(8,128)(2,1)}), (bf16[512,768]{1,0:T(8,128)(2,1)}, bf16[512,768]{1,0:T(8,128)(2,1)})) %all-reduce.7.cloned.1.call-update) | async-done | bytes 1572880 | tf_op jit(solution)/shard_map/psum | solution.py:40
  147.2 3.3 convolution_convert_fusion
  150.5 2.7 fusion.11
  153.2 0.0 all-reduce.5.cloned.1.call-update
  153.2 0.0 reduce-scatter.3.cloned.1.call-start
  153.3 2.0 convolution_convert_fusion.4
  155.3 0.0 reduce-scatter.3.cloned.1.call-update
  155.3 0.0 reduce-scatter.5.cloned.1.call-start
  155.4 3.7 convolution_convert_fusion.2
  159.1 0.0 reduce-scatter.5.cloned.1.call-update
  159.1 78.0 %all-reduce.5.cloned.1.call-done = (bf16[768,768]{0,1:T(8,128)(2,1)}, bf16[768,768]{0,1:T(8,128)(2,1)}) async-done(((bf16[768,768]{0,1:T(8,128)(2,1)}, bf16[768,768]{0,1:T(8,128)(2,1)}), (bf16[768,768]{0,1:T(8,128)(2,1)}, bf16[768,768]{0,1:T(8,128)(2,1)})) %all-reduce.5.cloned.1.call-update) | async-done | bytes 2359312 | tf_op jit(solution)/shard_map/psum | solution.py:59
  237.2 1.3 convert_multiply_fusion.6
  238.5 0.9 copy.9
  239.4 0.9 copy.10
  240.2 66.3 %reduce-scatter.3.cloned.1.call-done = bf16[32,768]{1,0:T(8,128)(2,1)} async-done(((bf16[512,768]{1,0:T(8,128)(2,1)}), bf16[32,768]{1,0:T(8,128)(2,1)}) %reduce-scatter.3.cloned.1.call-update) | async-done | bytes 49168 | tf_op jit(solution)/shard_map/reduce_scatter | solution.py:49
  306.6 68.1 %reduce-scatter.5.cloned.1.call-done = bf16[32,768]{1,0:T(8,128)(2,1)} async-done(((bf16[512,768]{1,0:T(8,128)(2,1)}), bf16[32,768]{1,0:T(8,128)(2,1)}) %reduce-scatter.5.cloned.1.call-update) | async-done | bytes 49168 | tf_op jit(solution)/shard_map/reduce_scatter | solution.py:52
  (9 shorter events, 0.0 us)
Async XLA Ops:
  7.2 49.9 %copy-start = (bf16[768,768]{1,0:T(8,128)(2,1)S(1)}, bf16[768,768]{1,0:T(8,128)(2,1)}, u32[]{:S(2)}) copy-start(bf16[768,768]{1,0:T(8,128)(2,1)} %param.6) | copy-start | bytes 3538948
  7.2 140.0 %all-reduce.7.cloned.1.call-start = ((), (), s32[]{:S(2)}) async-start(), calls=%async_computation.5 | async-start | bytes 3145728 | tf_op jit(solution)/shard_map/psum | solution.py:40
  7.2 48.2 %copy-start.1 = (bf16[768,768]{1,0:T(8,128)(2,1)S(1)}, bf16[768,768]{1,0:T(8,128)(2,1)}, u32[]{:S(2)}) copy-start(bf16[768,768]{1,0:T(8,128)(2,1)} %param.5) | copy-start | bytes 3538948
  58.8 178.4 %all-reduce.5.cloned.1.call-start = ((), (), s32[]{:S(2)}) async-start(), calls=%async_computation.4 | async-start | bytes 4718592 | tf_op jit(solution)/shard_map/psum | solution.py:59
  147.2 3.3 copy-start.3
  147.2 3.3 copy-start.4
  153.2 2.1 copy-start.2
  153.2 153.3 %reduce-scatter.3.cloned.1.call-start = ((), (), s32[]{:S(2)}) async-start(), calls=%async_computation.2 | async-start | bytes 835584 | tf_op jit(solution)/shard_map/reduce_scatter | solution.py:49
  155.3 219.4 %reduce-scatter.5.cloned.1.call-start = ((), (), s32[]{:S(2)}) async-start(), calls=%async_computation.3 | async-start | bytes 835584 | tf_op jit(solution)/shard_map/reduce_scatter | solution.py:52
Sparse Core Ops, SparseCore 0:
  58.9 88.2 all-reduce.6
  153.3 83.7 all-reduce.4
  240.6 65.9 reduce-scatter.2
  310.0 64.6 reduce-scatter.4
where the time goes:
time: 383 us; the launch traced here: 381 us
  waiting for transfers between devices  301 us (79%)
  blocking collectives  48.1 us (13%)
  matrix products  15.1 us (4%)
  between operations  13.8 us (4%)
    psum x1, waiting for transfers between devices, per_device(): lax.psum(up_part.astype(jnp.bfloat16), 'col').astype(jnp.float32)  88.3 us
    psum x1, waiting for transfers between devices, per_device(): lax.psum(up_local.astype(jnp.bfloat16), 'depth').astype(jnp.float32)  78 us
    reduce_scatter x1, waiting for transfers between devices, per_device(): lax.psum_scatter(input_part.astype(jnp.bfloat16), 'row', scatter_dimensio...  68.1 us
    reduce_scatter x1, waiting for transfers between devices, per_device(): lax.psum_scatter(out_part.astype(jnp.bfloat16), 'row', scatter_dimension=...  66.3 us
    all_gather x1, blocking collectives, per_device(): lax.all_gather(normed, 'row', axis=0, tiled=True)  27.8 us
    all_gather x1, blocking collectives, per_device(): lax.all_gather(out_grad, 'row', axis=0, tiled=True)  20.3 us
  transfers between devices with their start and end apart: 4, of which 4 were waited for; matrix products, arithmetic and copies ran while one was open for 2% of the time, Pallas kernels for 0%

commit v1 on v0

v1 whole, which is shorter than its diff:
```python
import functools
import math

import jax
import jax.numpy as jnp
from jax import lax
from jax.experimental import pallas as pl
from jax.experimental.pallas import tpu as pltpu
from jax.sharding import PartitionSpec as P

MESH = pl.DeviceIdType.MESH
BF16, F32 = jnp.bfloat16, jnp.float32
TOKEN_PARTS = 2
HIDDEN_PARTS = 6
ROLLED = True


def dot(left, right):
    return jnp.dot(left, right, preferred_element_type=F32)


def contract_last(left, right):
    return lax.dot_general(left, right, (((1,), (1,)), ((), ())), preferred_element_type=F32)


def contract_first(left, right):
    return lax.dot_general(left, right, (((0,), (0,)), ((), ())), preferred_element_type=F32)


def gelu_parts(value):
    coeff = math.sqrt(2.0 / math.pi)
    square = value * value
    tangent = jnp.tanh(coeff * (value + 0.044715 * square * value))
    half = 0.5 * (1.0 + tangent)
    slope = half + 0.5 * value * (1.0 - tangent * tangent) * coeff * (1.0 + 3.0 * 0.044715 * square)
    return value * half, slope


def add(first, second):
    return (first.astype(F32) + second.astype(F32)).astype(BF16)


def when(condition, action):
    if isinstance(condition, bool):
        if condition:
            action()
    else:
        pl.when(condition)(action)


def both(low, value, high):
    if isinstance(value, int):
        return low <= value < high
    return jnp.logical_and(value >= low, value < high)


def kernel(
    shape, factor,
    normed, up_weight, down_weight, out_grad,
    branch_out, normed_grad, up_grad, down_grad,
    tokens, tokens_t, perm, up_perm, down_perm,
    part, half_in, full_in, acts,
    grads, grads_in, rows, rows_in, ring, ring_half, ring_full, last, last_send, last_in,
    a_send, a_recv, z_send, z_recv, y_send, y_recv, r_send, r_recv,
):
    tn, hn, m, q, w, rt, n_depth = shape
    units = tn * hn
    slab = w // n_depth
    row, col, depth = lax.axis_index("row"), lax.axis_index("col"), lax.axis_index("depth")
    x, zl, core = row // 4, lax.rem(row // 2, 2), lax.rem(row, 2)

    def at_row(x_, zl_, core_):
        return x_ * 4 + zl_ * 2 + core_

    def ring_step(index, by, size):
        return lax.rem(index + by + size, size)

    right, left, opposite = (ring_step(col, by, 4) for by in (1, -1, 2))
    x_right, x_left, x_opposite = (ring_step(x, by, 4) for by in (1, -1, 2))
    to_right, to_left = {"col": right}, {"col": left}
    to_xr, to_xl = {"row": at_row(x_right, zl, core)}, {"row": at_row(x_left, zl, core)}
    to_zp, to_sib = {"row": at_row(x, 1 - zl, core)}, {"row": at_row(x, zl, 1 - core)}
    to_yr = {"depth": ring_step(depth, 1, n_depth)}
    to_yl = {"depth": ring_step(depth, -1, n_depth)}

    def copy(src, dst, send, recv, to):
        return pltpu.make_async_remote_copy(
            src_ref=src, dst_ref=dst, send_sem=send, recv_sem=recv, device_id=to, device_id_type=MESH
        )

    def got(dst, recv):
        copy(dst, dst, recv, recv, to_sib).wait_recv()

    def sent(src, send):
        copy(src, src, send, send, to_sib).wait_send()

    barrier = pltpu.get_barrier_semaphore()
    for to in (to_right, to_left, to_xr, to_xl, to_zp, to_sib, to_yr, to_yl):
        pl.semaphore_signal(barrier, inc=1, device_id=to, device_id_type=MESH)

    for t in range(tn):
        tokens[t, 0, row] = normed[t * rt : (t + 1) * rt, :]
        tokens[t, 1, row] = out_grad[t * rt : (t + 1) * rt, :]
    pl.semaphore_wait(barrier, 8)

    other = 1 - zl
    origin = [
        at_row(x, zl, core), at_row(x, other, core),
        at_row(x_left, zl, core), at_row(x_right, zl, core),
        at_row(x_left, other, core), at_row(x_right, other, core),
        at_row(x_opposite, zl, core), at_row(x_opposite, other, core),
    ]
    sib_origin = [at_row(x_, z_, 1 - core) for x_, z_ in (
        (x, zl), (x, other), (x_left, zl), (x_right, zl), (x_left, other), (x_right, other),
        (x_opposite, zl), (x_opposite, other))]

    def a_copy(t, src, to, send, recv):
        return copy(src, src, a_send.at[t, send], a_recv.at[t, recv], to)

    def piece(t, index):
        return tokens.at[t, :, origin[index]]

    def half(t, index, array):
        return tokens.at[t, array, origin[index]]

    def gather_1(t):
        a_copy(t, piece(t, 0), to_xr, 1, 1).start()
        a_copy(t, piece(t, 0), to_xl, 2, 2).start()
        a_copy(t, piece(t, 0), to_zp, 0, 0).start()
        a_copy(t, piece(t, 0), to_sib, 9, 9).start()

    def gather_2(t):
        got(piece(t, 1), a_recv.at[t, 0])
        a_copy(t, piece(t, 1), to_xr, 3, 3).start()
        a_copy(t, piece(t, 1), to_xl, 4, 4).start()
        got(piece(t, 2), a_recv.at[t, 1])
        a_copy(t, half(t, 2, 0), to_xr, 5, 5).start()
        got(piece(t, 3), a_recv.at[t, 2])
        a_copy(t, half(t, 3, 1), to_xl, 6, 6).start()
        for index in (1, 2, 3):
            a_copy(t, piece(t, index), to_sib, 9 + index, 9 + index).start()

    def gather_3(t):
        got(piece(t, 4), a_recv.at[t, 3])
        a_copy(t, half(t, 4, 0), to_xr, 7, 7).start()
        got(piece(t, 5), a_recv.at[t, 4])
        a_copy(t, half(t, 5, 1), to_xl, 8, 8).start()
        for index in (4, 5):
            a_copy(t, piece(t, index), to_sib, 9 + index, 9 + index).start()

    def gather_4(t):
        for index in (6, 7):
            got(half(t, index, 0), a_recv.at[t, 2 * index - 7])
            got(half(t, index, 1), a_recv.at[t, 2 * index - 6])
            a_copy(t, piece(t, index), to_sib, 9 + index, 9 + index).start()

    def gather_5(t):
        for index in range(8):
            got(tokens.at[t, :, sib_origin[index]], a_recv.at[t, 9 + index])
        tokens_t[t] = tokens[t, 0].reshape(m, -1).T
        for send, index in ((0, 0), (1, 0), (2, 0), (3, 1), (4, 1)):
            sent(piece(t, index), a_send.at[t, send])
        for send, index, array in ((5, 2, 0), (6, 3, 1), (7, 4, 0), (8, 5, 1)):
            sent(half(t, index, array), a_send.at[t, send])
        for index in range(8):
            sent(piece(t, index), a_send.at[t, 9 + index])

    gather_1(0)
    extent = up_weight.shape[1]
    for h in range(hn):
        inner = lax.broadcasted_iota(jnp.int32, (extent, w), 1)
        wanted = (inner // slab) * (extent // n_depth) + h * slab + lax.rem(inner, slab)
        perm[h] = jnp.where(lax.broadcasted_iota(jnp.int32, (extent, w), 0) == wanted, 1.0, 0.0).astype(BF16)
        up_perm[h] = dot(up_weight[...], perm[h]).astype(BF16)
        for d in range(n_depth):
            base = d * (extent // n_depth) + h * slab
            down_perm[h, d * slab : (d + 1) * slab, :] = down_weight[base : base + slab, :]
    gather_2(0)
    for t in range(1, tn):
        gather_1(t)
    gather_3(0)
    for t in range(1, tn):
        gather_2(t)
    gather_4(0)
    for t in range(1, tn):
        gather_3(t)
    gather_5(0)

    def split(unit):
        return unit // hn, unit % hn

    def stage_f(u):
        t, h = split(u)
        up = dot(tokens[t, 0].reshape(m, -1), up_perm[h]).astype(BF16)
        part[u, :, 0] = up.reshape(4, q, w)
        back = contract_last(tokens[t, 1].reshape(m, -1), down_perm[h]).astype(BF16)
        part[u, :, 1] = back.reshape(4, q, w)
        copy(part.at[u, opposite, 0], half_in.at[u, 0], z_send.at[u, 0], z_recv.at[u, 0], to_right).start()
        copy(part.at[u, opposite, 1], half_in.at[u, 1], z_send.at[u, 1], z_recv.at[u, 1], to_left).start()

    def stage_r1(u):
        got(half_in.at[u, 0], z_recv.at[u, 0])
        part[u, right, 0] = add(part[u, right, 0], half_in[u, 0])
        copy(part.at[u, right], full_in.at[u, 0], z_send.at[u, 2], z_recv.at[u, 2], to_right).start()
        got(half_in.at[u, 1], z_recv.at[u, 1])
        part[u, left, 1] = add(part[u, left, 1], half_in[u, 1])
        copy(part.at[u, left], full_in.at[u, 1], z_send.at[u, 3], z_recv.at[u, 3], to_left).start()

    def stage_r2(u):
        got(full_in.at[u, 0], z_recv.at[u, 2])
        got(full_in.at[u, 1], z_recv.at[u, 3])
        total = part[u, col].astype(F32) + full_in[u, 0].astype(F32) + full_in[u, 1].astype(F32)
        active, slope = gelu_parts(total[0])
        acts[u, 0, col] = active.astype(BF16)
        acts[u, 1, col] = (total[1] * slope).astype(BF16)
        mine = acts.at[u, :, col]
        copy(mine, mine, z_send.at[u, 4], z_recv.at[u, 4], to_right).start()
        copy(mine, mine, z_send.at[u, 5], z_recv.at[u, 5], to_left).start()
        sent(part.at[u, opposite, 0], z_send.at[u, 0])
        sent(part.at[u, opposite, 1], z_send.at[u, 1])

    def stage_a1(u):
        got(acts.at[u, :, left], z_recv.at[u, 4])
        copy(acts.at[u, 0, left], acts.at[u, 0, left], z_send.at[u, 6], z_recv.at[u, 6], to_right).start()
        got(acts.at[u, :, right], z_recv.at[u, 5])
        copy(acts.at[u, 1, right], acts.at[u, 1, right], z_send.at[u, 7], z_recv.at[u, 7], to_left).start()
        sent(part.at[u, right], z_send.at[u, 2])
        sent(part.at[u, left], z_send.at[u, 3])

    def y_copies(h, step):
        if step == 0:
            far = ring_step(depth, n_depth // 2, n_depth)
            pairs = (
                (grads.at[h, far, 0], grads_in.at[h, 0, 0, 0]),
                (grads.at[h, far, 1], grads_in.at[h, 0, 1, 1]),
            )
        else:
            away = n_depth // 2 - step
            pairs = (
                (grads.at[h, ring_step(depth, away, n_depth)], grads_in.at[h, step, 0]),
                (grads.at[h, ring_step(depth, -away, n_depth)], grads_in.at[h, step, 1]),
            )
        return tuple(
            copy(src, dst, y_send.at[h, step, way], y_recv.at[h, step, way], to)
            for way, ((src, dst), to) in enumerate(zip(pairs, (to_yr, to_yl)))
        )

    y_steps = n_depth // 2

    def stage_y(h, step):
        before = y_copies(h, step - 1)
        if step == y_steps:
            before[0].wait_recv()
            before[1].wait_recv()
            total = (
                grads[h, depth].astype(F32) + grads_in[h, step - 1, 0].astype(F32) + grads_in[h, step - 1, 1].astype(F32)
            ) * factor
            down_grad[pl.ds(pl.multiple_of(h * slab, slab), slab), :] = total[1]
            block = jnp.concatenate([total[0, :, j * w : (j + 1) * w] for j in range(hn)], axis=0)
            high = block.astype(BF16)
            low = (block - high.astype(F32)).astype(BF16)
            spread = contract_last(high, perm[h]) + contract_last(low, perm[h])
            up_grad[...] = up_grad[...] + spread
        else:
            now = y_copies(h, step)
            for way, sign in ((0, 1), (1, -1)):
                before[way].wait_recv()
                owner = ring_step(depth, sign * (y_steps - step), n_depth)
                if step == 1:
                    grads[h, owner, way] = add(grads[h, owner, way], grads_in[h, 0, way, way])
                else:
                    grads[h, owner] = add(grads[h, owner], grads_in[h, step - 1, way])
                now[way].start()
        before[0].wait_send()
        before[1].wait_send()

    def row_copies(t, step):
        if step == 0:
            return (copy(rows.at[t, :, :, 1 - core], rows_in.at[t], r_send.at[t, 0], r_recv.at[t, 0], to_sib),)
        if step == 1:
            return (
                copy(ring.at[t, x_opposite, 0], ring_half.at[t, 0], r_send.at[t, 1], r_recv.at[t, 1], to_xr),
                copy(ring.at[t, x_opposite, 1], ring_half.at[t, 1], r_send.at[t, 2], r_recv.at[t, 2], to_xl),
            )
        if step == 2:
            return (
                copy(ring.at[t, x_right], ring_full.at[t, 0], r_send.at[t, 3], r_recv.at[t, 3], to_xr),
                copy(ring.at[t, x_left], ring_full.at[t, 1], r_send.at[t, 4], r_recv.at[t, 4], to_xl),
            )
        return (copy(last_send.at[t], last_in.at[t], r_send.at[t, 5], r_recv.at[t, 5], to_zp),)

    def stage_row(t, step):
        before = row_copies(t, step - 1)
        now = row_copies(t, step) if step < 4 else ()
        if step == 1:
            before[0].wait_recv()
            for xs in range(4):
                for array in range(2):
                    ring[t, xs, array] = add(rows[t, array, 2 * xs : 2 * xs + 2, core], rows_in[t, array, 2 * xs : 2 * xs + 2])
        elif step == 2:
            before[0].wait_recv()
            ring[t, x_right, 0] = add(ring[t, x_right, 0], ring_half[t, 0])
            before[1].wait_recv()
            ring[t, x_left, 1] = add(ring[t, x_left, 1], ring_half[t, 1])
        elif step == 3:
            before[0].wait_recv()
            before[1].wait_recv()
            last[t] = ring[t, x].astype(F32) + ring_full[t, 0].astype(F32) + ring_full[t, 1].astype(F32)
            last_send[t] = last[t, :, 1 - zl].astype(BF16)
        else:
            before[0].wait_recv()
            total = (last[t, :, zl] + last_in[t].astype(F32)).astype(BF16)
            here = pl.ds(t * rt if isinstance(t, int) else pl.multiple_of(t * rt, rt), rt)
            branch_out[here, :] = total[0]
            normed_grad[here, :] = total[1]
        for one in now:
            one.start()
        for one in before:
            one.wait_send()

    def stage_b(u):
        t, h = split(u)
        got(acts.at[u, 0, opposite], z_recv.at[u, 6])
        got(acts.at[u, 1, opposite], z_recv.at[u, 7])

        def weight_grads():
            up = sum(dot(tokens_t[s], acts[s * hn + h, 1].reshape(m, w)) for s in range(tn)).astype(BF16)
            down = sum(
                contract_first(acts[s * hn + h, 0].reshape(m, w), tokens[s, 1].reshape(m, -1)) for s in range(tn)
            ).astype(BF16)
            for d in range(n_depth):
                for j in range(hn):
                    base = d * slab * hn + j * slab
                    grads[h, d, 0, :, j * w : (j + 1) * w] = up[base : base + slab, :]
                grads[h, d, 1] = down[d * slab : (d + 1) * slab, :]
            for one in y_copies(h, 0):
                one.start()

        def token_sums():
            active = jnp.concatenate([acts[t * hn + i, 0].reshape(m, w) for i in range(hn)], axis=1)
            out = dot(active, down_perm[...].reshape(hn * w, -1)).astype(BF16)
            rows[t, 0] = out.reshape(8, 2, rt, -1)
            cotangent = jnp.concatenate([acts[t * hn + i, 1].reshape(m, w) for i in range(hn)], axis=1)
            weight = jnp.concatenate([up_perm[i] for i in range(hn)], axis=1)
            back = contract_last(cotangent, weight).astype(BF16)
            rows[t, 1] = back.reshape(8, 2, rt, -1)
            for one in row_copies(t, 0):
                one.start()

        when(h == hn - 1, token_sums)
        when(t == tn - 1, weight_grads)
        sent(acts.at[u, :, col], z_send.at[u, 4])
        sent(acts.at[u, :, col], z_send.at[u, 5])
        sent(acts.at[u, 0, left], z_send.at[u, 6])
        sent(acts.at[u, 1, right], z_send.at[u, 7])

    up_grad[...] = jnp.zeros_like(up_grad)
    first_y = (tn - 1) * hn + 4

    def turn(k):
        for t in range(1, tn):
            when(k == (t - 1) * hn + 1, functools.partial(gather_4, t))
            when(k == t * hn, functools.partial(gather_5, t))
        when(both(0, k, units), lambda: stage_f(k))
        when(both(1, k, units + 1), lambda: stage_r1(k - 1))
        when(both(2, k, units + 2), lambda: stage_r2(k - 2))
        when(both(3, k, units + 3), lambda: stage_a1(k - 3))
        for step in range(1, 5):
            for t in range(tn):
                when(k == t * hn + hn + 3 + step, functools.partial(stage_row, t, step))
        for step in range(1, y_steps + 1):
            when(
                both(first_y + step, k, first_y + step + hn),
                lambda step=step: stage_y(k - first_y - step, step),
            )
        when(both(4, k, units + 4), lambda: stage_b(k - 4))

    turns = units + 4 + max(4, y_steps)
    if ROLLED:
        pl.loop(0, turns)(turn)
    else:
        for k in range(turns):
            turn(k)


def solution(mesh):
    n_row, n_col, n_depth = (mesh.shape[name] for name in ("row", "col", "depth"))
    tn, hn = TOKEN_PARTS, HIDDEN_PARTS

    def per_device(normed, up_weight, down_weight, out_grad):
        block, width = normed.shape
        hidden = up_weight.shape[1]
        rt, w = block // tn, hidden // hn
        m = rt * n_row
        q = m // n_col
        slab = w // n_depth
        units = tn * hn
        factor = 1.0 / math.sqrt(block * n_row * n_depth)
        dma = pltpu.SemaphoreType.DMA
        vmem = pltpu.VMEM
        whole = pl.BlockSpec(memory_space=pltpu.VMEM)
        return pl.pallas_call(
            functools.partial(kernel, (tn, hn, m, q, w, rt, n_depth), factor),
            out_shape=(
                jax.ShapeDtypeStruct((block, width), BF16),
                jax.ShapeDtypeStruct((block, width), BF16),
                jax.ShapeDtypeStruct((width // n_depth, hidden), F32),
                jax.ShapeDtypeStruct((hidden // n_depth, width), F32),
            ),
            in_specs=[whole] * 4,
            out_specs=[whole] * 4,
            scratch_shapes=[
                vmem((tn, 2, n_row, rt, width), BF16),
                vmem((tn, width, m), BF16),
                vmem((hn, hidden, w), BF16),
                vmem((hn, width, w), BF16),
                vmem((hn, w, width), BF16),
                vmem((units, n_col, 2, q, w), BF16),
                vmem((units, 2, q, w), BF16),
                vmem((units, 2, 2, q, w), BF16),
                vmem((units, 2, n_col, q, w), BF16),
                vmem((hn, n_depth, 2, slab, width), BF16),
                vmem((hn, n_depth // 2, 2, 2, slab, width), BF16),
                vmem((tn, 2, n_row // 2, 2, rt, width), BF16),
                vmem((tn, 2, n_row // 2, rt, width), BF16),
                vmem((tn, 4, 2, 2, rt, width), BF16),
                vmem((tn, 2, 2, rt, width), BF16),
                vmem((tn, 2, 2, 2, rt, width), BF16),
                vmem((tn, 2, 2, rt, width), F32),
                vmem((tn, 2, rt, width), BF16),
                vmem((tn, 2, rt, width), BF16),
                dma((tn, 17)), dma((tn, 17)),
                dma((units, 8)), dma((units, 8)),
                dma((hn, n_depth // 2, 2)), dma((hn, n_depth // 2, 2)),
                dma((tn, 6)), dma((tn, 6)),
            ],
            compiler_params=pltpu.CompilerParams(
                collective_id=0, has_side_effects=True, vmem_limit_bytes=56 * 1024 * 1024
            ),
            cost_estimate=pl.CostEstimate(flops=4_000_000_000, bytes_accessed=4_000_000, transcendentals=400_000),
        )(normed, up_weight, down_weight, out_grad)

    return jax.shard_map(
        per_device,
        mesh=mesh,
        in_specs=(P(("depth", "row"), "col"), P("col", "row"), P("row", "col"), P(("depth", "row"), "col")),
        out_specs=(
            P(("depth", "row"), "col"),
            P(("depth", "row"), "col"),
            P(("col", "depth"), "row"),
            P(("row", "depth"), "col"),
        ),
        check_vma=False,
    )
```

time: 383 us -> 125 us (0.33)
  waiting for transfers between devices: 301 us -> 0 us
  Pallas kernels: 0 us -> 116 us
  blocking collectives: 48.1 us -> 0 us
  matrix products: 15.1 us -> 0 us
  between operations: 13.8 us -> 0.64 us
  local copies, waits for them, and re-layouts: 1.78 us -> 6.23 us
    psum x2 -> x0, waiting for transfers between devices: 166 us -> none  [the longest x1 88.3 us: per_device(): lax.psum(up_part.astype(jnp.bfloat16), 'col').astype(jnp.float32)]
    reduce_scatter x2 -> x0, waiting for transfers between devices: 134 us -> none  [the longest x1 68.1 us: per_device(): lax.psum_scatter(input_part.astype(jnp.bfloat16), 'row', scatter_dimensio...]
    pallas_call x0 -> x1, Pallas kernels: none -> 116 us  [per_device(): pl.pallas_call(functools.partial(kernel, (tn, hn, m, q, w, rt, n_depth),...]
    all_gather x2 -> x0, blocking collectives: 48.1 us -> none  [the longest x1 27.8 us: per_device(): lax.all_gather(normed, 'row', axis=0, tiled=True)]
    dot_general x6 -> x0, matrix products: 15.1 us -> none  [the longest x2 6 us: contract_first(): lax.dot_general(left, right, (((0,), (0,)), ((), ())), preferred_element_...]
    unnamed x12 -> x4, local copies, waits for them, and re-layouts: 1.78 us -> 6.23 us
  transfers between devices with their start and end apart: 4 -> 0, of which waited for: 4 -> 0; matrix products, arithmetic and copies ran while one was open for 2% -> 0% of each run, Pallas kernels for 0% -> 0%
where the time goes in v1:
time: 125 us; the launch traced here: 123 us
  Pallas kernels  116 us (93%)
  local copies, waits for them, and re-layouts  6.23 us (5%)
    pallas_call x1, Pallas kernels, per_device(): pl.pallas_call(functools.partial(kernel, (tn, hn, m, q, w, rt, n_depth),...  116 us
    unnamed x4, local copies, waits for them, and re-layouts  6.23 us

profile of v1, /device:TPU:1, one launch (start us, length us, event | category | flops | bytes accessed | tf_op | source)
XLA Modules:
  0.0 123.2 jit_solution(539572799552165062)
XLA Ops:
  0.6 116.3 %shard_map.75 = (bf16[32,768]{1,0:T(8,128)(2,1)}, bf16[32,768]{1,0:T(8,128)(2,1)}, f32[96,768]{1,0:T(8,128)}, f32[96,768]{1,0:T(8,128)}) custom-call(bf16[32,768]{1,0:T(8,128)(2,1)} %normed.1, bf16[768,768]{1,0:T(8,128)(2,1)} %up_weight.1, bf16[768,768]{1,0:T(8,128)(2,1)} %down_weight.1, bf16[32,768]{1,0:T(8,128)(2,1)} %out_grad.1), custom_call_target="tpu_custom_call" | custom-call | flops 4000000000 | bytes 4000000 | tf_op jit(solution)/shard_map/pallas_call | solution.py:402
  116.9 1.4 %copy.12 = bf16[32,768]{1,0:T(8,128)(2,1)} copy(bf16[32,768]{1,0:T(8,128)(2,1)} %get-tuple-element.8) | data formatting | bytes 98304
  118.4 1.4 %copy.13 = bf16[32,768]{1,0:T(8,128)(2,1)} copy(bf16[32,768]{1,0:T(8,128)(2,1)} %get-tuple-element.9) | data formatting | bytes 98304
  119.8 1.7 %copy.14 = f32[96,768]{1,0:T(8,128)} copy(f32[96,768]{1,0:T(8,128)} %get-tuple-element.10) | data formatting | bytes 589824
  121.5 1.7 %copy.15 = f32[96,768]{1,0:T(8,128)} copy(f32[96,768]{1,0:T(8,128)} %get-tuple-element.11) | data formatting | bytes 589824

commit v2 on v0

v2 whole, which is shorter than its diff:
```python
import functools
import math

import jax
import jax.numpy as jnp
from jax import lax
from jax.experimental import pallas as pl
from jax.experimental.pallas import tpu as pltpu
from jax.sharding import PartitionSpec as P

MESH = pl.DeviceIdType.MESH
BF16, F32 = jnp.bfloat16, jnp.float32
NX, NZ, NC = 4, 8, 4


def dot(left, right):
    return jnp.dot(left, right, preferred_element_type=F32)


def contract_last(left, right):
    return lax.dot_general(left, right, (((1,), (1,)), ((), ())), preferred_element_type=F32)


def contract_first(left, right):
    return lax.dot_general(left, right, (((0,), (0,)), ((), ())), preferred_element_type=F32)


def gelu_parts(value):
    coeff = math.sqrt(2.0 / math.pi)
    square = value * value
    tangent = jnp.tanh(coeff * (value + 0.044715 * square * value))
    half = 0.5 * (1.0 + tangent)
    slope = half + 0.5 * value * (1.0 - tangent * tangent) * coeff * (1.0 + 3.0 * 0.044715 * square)
    return value * half, slope


def add(first, second):
    return (first.astype(F32) + second.astype(F32)).astype(BF16)


def wrap(index, by, size):
    return lax.rem(index + by + size, size)


def kernel(
    shape, factor,
    normed, up_weight, down_weight, out_grad,
    branch_out, normed_grad, up_grad, down_grad,
    tokens, perm, w_own, weights, up_share,
    act, pre_grad, grads, grads_sib, grads_in, grads_own, grads_back,
    out, out_half, out_full, ring, ring_in,
    t_send, t_recv, tx_send, tx_recv, a_send, a_recv, w_send, w_recv, s_send, s_recv,
    g_send, g_recv, y_send, y_recv, b_send, b_recv, x_send, x_recv, z_send, z_recv,
):
    block, m, share, slab, ny = shape
    width = normed.shape[1]
    hidden = up_weight.shape[1]
    lanes = width // 2
    row, k, depth = lax.axis_index("row"), lax.axis_index("col"), lax.axis_index("depth")
    x, zl, core = row // 4, lax.rem(row // 2, 2), lax.rem(row, 2)
    z = 2 * k + zl
    holder, half_of = k // 2, lax.rem(k, 2)

    def at(x_, z_, core_):
        return {"row": x_ * 4 + lax.rem(z_, 2) * 2 + core_, "col": z_ // 2}

    def peer(k_, core_):
        return {"row": x * 4 + zl * 2 + core_, "col": k_}

    x_right, x_left, x_far = wrap(x, 1, NX), wrap(x, -1, NX), wrap(x, 2, NX)
    to_x = (at(x_right, z, core), at(x_left, z, core))
    to_z = (at(x, wrap(z, 1, NZ), core), at(x, wrap(z, -1, NZ), core))
    to_y = ({"depth": wrap(depth, 1, ny)}, {"depth": wrap(depth, -1, ny)})
    to_sib = peer(k, 1 - core)

    def copy(src, dst, send, recv, to):
        return pltpu.make_async_remote_copy(
            src_ref=src, dst_ref=dst, send_sem=send, recv_sem=recv, device_id=to, device_id_type=MESH
        )

    def got(dst, recv):
        copy(dst, dst, recv, recv, to_sib).wait_recv()

    def sent(src, send):
        copy(src, src, send, send, to_sib).wait_send()

    barrier = pltpu.get_barrier_semaphore()
    others = [peer(wrap(k, by, NC), core_) for by in (1, 2, 3) for core_ in (0, 1)]
    partners = (*to_x, *to_z, *to_y, to_sib, *others)
    for to in partners:
        pl.semaphore_signal(barrier, inc=1, device_id=to, device_id_type=MESH)
    tokens[0, k, x, zl] = normed[...]
    tokens[1, k, x, zl] = out_grad[...]
    pl.semaphore_wait(barrier, len(partners))

    events = []

    def on(time, action, *args):
        events.append((time, len(events), functools.partial(action, *args)))

    def run():
        for _, _, action in sorted(events, key=lambda e: e[:2]):
            action()
        events.clear()

    def slot_ref(x_, slot):
        return tokens.at[:, slot // 2, x_, lax.rem(slot, 2)]

    def slot_half(x_, slot, array):
        return tokens.at[array, slot // 2, x_, lax.rem(slot, 2)]

    def tz_copy(step, way):
        slot = wrap(z, -(1 if way == 0 else -1) * (step - 1), NZ)
        ref = slot_ref(x, slot) if step < NZ // 2 else slot_half(x, slot, way)
        return copy(ref, ref, t_send.at[step - 1, way], t_recv.at[step - 1, way], to_z[way])

    offsets = (0, -1, 1, -2, 2, -3, 3, 4)

    def tx_copy(n, step, way):
        slot = wrap(z, offsets[n], NZ)
        if step == 0:
            ref = slot_ref(x, slot)
        else:
            ref = slot_half(x_left if way == 0 else x_right, slot, way)
        return copy(ref, ref, tx_send.at[n, step, way], tx_recv.at[n, step, way], to_x[way])

    def tokens_z(step):
        for way in range(2):
            if step > 1:
                slot = wrap(z, -(1 if way == 0 else -1) * (step - 1), NZ)
                full = step - 1 < NZ // 2
                got(slot_ref(x, slot) if full else slot_half(x, slot, way), t_recv.at[step - 2, way])
            if step <= NZ // 2:
                tz_copy(step, way).start()
            if 1 < step <= NZ // 2:
                for way_x in range(2):
                    tx_copy(2 * (step - 1) - 1 + way, 0, way_x).start()
        if step == 1:
            for way_x in range(2):
                tx_copy(0, 0, way_x).start()
        if step == NZ // 2 + 1:
            for way_x in range(2):
                tx_copy(7, 0, way_x).start()

    def tokens_x(n, step):
        slot = wrap(z, offsets[n], NZ)
        for way in range(2):
            if step == 1:
                got(slot_ref(x_left if way == 0 else x_right, slot), tx_recv.at[n, 0, way])
                tx_copy(n, 1, way).start()
            else:
                got(slot_half(x_far, slot, way), tx_recv.at[n, 1, way])

    def prepare():
        shift = slab.bit_length() - 1
        inner = lax.broadcasted_iota(jnp.int32, (hidden, share), 1)
        index = (inner // slab) * (hidden // ny) + lax.rem(inner, slab)
        place = lax.broadcasted_iota(jnp.int32, (hidden, share), 0)
        for h in range(2):
            perm[:, h * share : (h + 1) * share] = jnp.where(place == index + h * slab, 1.0, 0.0).astype(BF16)
        rows = hidden // ny
        mixed = dot(up_weight[pl.ds(pl.multiple_of(depth * rows, rows), rows), :], perm[...]).astype(BF16)
        for h in range(2):
            for j in range(2):
                w_own[h, 0, :, j * share : (j + 1) * share] = mixed[j * slab : (j + 1) * slab, h * share : (h + 1) * share]
            w_own[h, 1] = down_weight[pl.ds(pl.multiple_of(depth * rows + h * slab, slab), slab), :]
            to = 2 * core + h

            @pl.when(to != k)
            def _():
                for array in range(2):
                    copy(w_own.at[h, array], weights.at[array, k, depth], a_send.at[h, array], a_recv.at[k], peer(to, array)).start()

        @pl.when(core == holder)
        def _():
            for d in range(ny):
                weights[1, k, d] = down_weight[pl.ds(pl.multiple_of(d * rows + half_of * slab, slab), slab), :]
            here = pl.ds(pl.multiple_of(half_of * share, share), share)
            up_share[k] = dot(up_weight[...], perm[:, here]).astype(BF16)
            own_copies()[0].start()
            own_copies()[1].start()

    def own_copies():
        return (
            copy(weights.at[1, k], weights.at[1, k], s_send.at[3], s_recv.at[3], to_sib),
            copy(up_share.at[k], up_share.at[k], s_send.at[4], s_recv.at[4], to_sib),
        )

    def w_ref(j, slot):
        return weights.at[core, wrap(k, 1 + j, NC), slot]

    def w_half(j, slot, way):
        return weights.at[core, wrap(k, 1 + j, NC), slot, :, way * lanes : (way + 1) * lanes]

    def w_copy(j, step, way):
        slot = wrap(depth, -(1 if way == 0 else -1) * (step - 1), ny)
        ref = w_ref(j, slot) if step < ny // 2 else w_half(j, slot, way)
        return copy(ref, ref, w_send.at[j, step - 1, way], w_recv.at[j, step - 1, way], to_y[way])

    def w_sib(j):
        ref = weights.at[core, wrap(k, 1 + j, NC)]
        return copy(ref, ref, s_send.at[j], s_recv.at[j], to_sib)

    def weights_y(j, step):
        if step == 1:
            got(w_ref(j, depth), a_recv.at[wrap(k, 1 + j, NC)])
        for way in range(2):
            if step > 1:
                slot = wrap(depth, -(1 if way == 0 else -1) * (step - 1), ny)
                got(w_ref(j, slot) if step - 1 < ny // 2 else w_half(j, slot, way), w_recv.at[j, step - 2, way])
            if step <= ny // 2:
                w_copy(j, step, way).start()
        if step == ny // 2 + 1:
            w_sib(j).start()

    def weights_in(j):
        c = wrap(k, 1 + j, NC)
        got(weights.at[1 - core, c], s_recv.at[j])
        for d in range(ny):
            for i in range(2):
                base = (2 * d + i) * slab
                up_share[c, base : base + slab, :] = weights[0, c, d, :, i * share : (i + 1) * share]

    def own_in():
        @pl.when(core != holder)
        def _():
            got(weights.at[1, k], s_recv.at[3])
            got(up_share.at[k], s_recv.at[4])

        @pl.when(core == holder)
        def _():
            for one in own_copies():
                one.wait_send()

    tokens_z(1)
    prepare()
    for step in range(2, NZ // 2 + 2):
        on(3.5 * (step - 1), tokens_z, step)
    for n in range(8):
        on(3.2 * n + 4, tokens_x, n, 1)
        on(3.2 * n + 7.5, tokens_x, n, 2)
    for j in range(NC - 1):
        for step in range(1, ny // 2 + 2):
            on(5.5 + 5.5 * j + 3.4 * (step - 1), weights_y, j, step)
        on(5.5 + 5.5 * j + 3.4 * 4 + 2.5, weights_in, j)
    on(16, own_in)
    run()

    up = sum(dot(tokens[0, c].reshape(m, width), up_share[c]) for c in range(NC))
    back = sum(contract_last(tokens[1, c].reshape(m, width), weights[1, c].reshape(share, width)) for c in range(NC))
    active, slope = gelu_parts(up)
    act[...] = active.astype(BF16)
    pre_grad[...] = (back * slope).astype(BF16)

    order = tuple((dc, flip) for dc in (2, 1, 3, 0) for flip in (0, 1))

    def place(n):
        dc, flip = order[n]
        return wrap(k, dc, NC), (zl if flip == 0 else 1 - zl)

    def out_copy(n, step, way):
        c, zs = place(n)
        if step == 0:
            return copy(out.at[x_far, c, zs, way], out_half.at[n, way], x_send.at[n, 0, way], x_recv.at[n, 0, way], to_x[way])
        to_ = x_right if way == 0 else x_left
        return copy(out.at[to_, c, zs], out_full.at[n, way], x_send.at[n, 1, way], x_recv.at[n, 1, way], to_x[way])

    def grad_sib(i):
        c = wrap(k, order[2 * i][0], NC)
        return copy(grads.at[1 - core, c], grads_sib.at[c], g_send.at[i], g_recv.at[i], to_sib)

    def produce(i):
        c = wrap(k, order[2 * i][0], NC)
        branch = dot(act[...], weights[1, c].reshape(share, width)).astype(BF16)
        out[:, c, :, 0] = branch.reshape(NX, 2, block, width)
        inputs = contract_last(pre_grad[...], up_share[c]).astype(BF16)
        out[:, c, :, 1] = inputs.reshape(NX, 2, block, width)
        for n in (2 * i, 2 * i + 1):
            for way in range(2):
                out_copy(n, 0, way).start()
        down = contract_first(act[...], tokens[1, c].reshape(m, width)).astype(BF16)
        grads[1, c] = down.reshape(ny, slab, width)
        upper = contract_first(tokens[0, c].reshape(m, width), pre_grad[...]).astype(BF16)
        for d in range(ny):
            for j in range(2):
                base = (2 * d + j) * slab
                grads[0, c, d, :, j * share : (j + 1) * share] = upper[base : base + slab, :]
        grad_sib(i).start()

    for i in range(NC):
        produce(i)

    def out_x(n, step):
        c, zs = place(n)
        for way in range(2):
            out_copy(n, step - 1, way).wait_recv()
            if step == 1:
                to_ = x_right if way == 0 else x_left
                out[to_, c, zs, way] = add(out[to_, c, zs, way], out_half[n, way])
                out_copy(n, 1, way).start()
        if step == 2:
            total = out[x, c, zs].astype(F32) + out_full[n, 0].astype(F32) + out_full[n, 1].astype(F32)
            ring[2 * c + zs] = total.astype(BF16)

    def z_copy(step, way):
        slot = wrap(z, (1 if way == 0 else -1) * (NZ // 2 - step), NZ)
        if step == 0:
            return copy(ring.at[slot, way], ring_in.at[0, way, way], z_send.at[0, way], z_recv.at[0, way], to_z[way])
        return copy(ring.at[slot], ring_in.at[step, way], z_send.at[step, way], z_recv.at[step, way], to_z[way])

    def out_z(step):
        if step == NZ // 2:
            for way in range(2):
                z_copy(step - 1, way).wait_recv()
            total = ring[z].astype(F32) + ring_in[step - 1, 0].astype(F32) + ring_in[step - 1, 1].astype(F32)
            branch_out[...] = total[0].astype(BF16)
            normed_grad[...] = total[1].astype(BF16)
            return
        for way in range(2):
            slot = wrap(z, (1 if way == 0 else -1) * (NZ // 2 - step), NZ)
            if step > 0:
                z_copy(step - 1, way).wait_recv()
            if step == 1:
                ring[slot, way] = add(ring[slot, way], ring_in[0, way, way])
            elif step > 1:
                ring[slot] = add(ring[slot], ring_in[step - 1, way])
            z_copy(step, way).start()

    def y_copy(i, step, way):
        c = wrap(k, order[2 * i][0], NC)
        slot = wrap(depth, (1 if way == 0 else -1) * (ny // 2 - step), ny)
        src, dst = grads.at[core, c, slot], grads_in.at[i, step, way]
        if step == 0:
            src = grads.at[core, c, slot, :, way * lanes : (way + 1) * lanes]
            dst = grads_in.at[i, 0, way, :, way * lanes : (way + 1) * lanes]
        return copy(src, dst, y_send.at[i, step, way], y_recv.at[i, step, way], to_y[way])

    def back_copy(i):
        dc = order[2 * i][0]
        c = wrap(k, dc, NC)
        return copy(grads_own.at[i], grads_back.at[core, half_of], b_send.at[i], b_recv.at[core, half_of], peer(c, holder))

    def grads_y(i, step):
        c = wrap(k, order[2 * i][0], NC)
        if step == 0:
            got(grads_sib.at[c], g_recv.at[i])
            grads[core, c] = add(grads[core, c], grads_sib[c])
        if step < ny // 2:
            for way in range(2):
                slot = wrap(depth, (1 if way == 0 else -1) * (ny // 2 - step), ny)
                cut = slice(way * lanes, (way + 1) * lanes)
                if step > 0:
                    y_copy(i, step - 1, way).wait_recv()
                if step == 1:
                    grads[core, c, slot, :, cut] = add(grads[core, c, slot, :, cut], grads_in[i, 0, way, :, cut])
                elif step > 1:
                    grads[core, c, slot] = add(grads[core, c, slot], grads_in[i, step - 1, way])
                y_copy(i, step, way).start()
            return
        for way in range(2):
            y_copy(i, step - 1, way).wait_recv()
        total = grads[core, c, depth].astype(F32) + grads_in[i, step - 1, 0].astype(F32) + grads_in[i, step - 1, 1].astype(F32)
        grads_own[i] = total.astype(BF16)
        if order[2 * i][0] != 0:
            back_copy(i).start()
        else:
            @pl.when(core == holder)
            def _():
                grads_back[core, half_of] = grads_own[i]

            @pl.when(core != holder)
            def _():
                back_copy(i).start()

    for i in range(NC):
        for step in range(ny // 2 + 1):
            on(5 + 5.8 * i + 4 * step, grads_y, i, step)
    for n in range(8):
        on(3.5 + 3.2 * n, out_x, n, 1)
        on(8.5 + 3.2 * n, out_x, n, 2)
    on(8.6, out_z, 0)
    on(8.6 + 3.2 * 5, out_z, 1)
    on(8.7 + 3.2 * 5 + 3.5, out_z, 2)
    on(8.7 + 3.2 * 7 + 3.5, out_z, 3)
    on(8.7 + 3.2 * 7 + 7, out_z, 4)
    run()

    for h in range(2):
        for array in range(2):
            local = jnp.logical_and(2 * core + h == k, core == array)

            @pl.when(jnp.logical_not(local))
            def _():
                got(grads_back.at[array, h], b_recv.at[array, h])

    for h in range(2):
        down_grad[h * slab : (h + 1) * slab, :] = grads_back[1, h].astype(F32) * factor
    halves = [
        jnp.concatenate([grads_back[0, h, :, j * share : (j + 1) * share] for j in range(2)], axis=0) for h in range(2)
    ]
    up_grad[...] = contract_last(jnp.concatenate(halves, axis=1), perm[...]) * factor

    for way in range(2):
        for step in range(1, NZ // 2 + 1):
            tz_copy(step, way).wait_send()
        for n in range(8):
            for step in range(2):
                tx_copy(n, step, way).wait_send()
                out_copy(n, step, way).wait_send()
        for j in range(NC - 1):
            for step in range(1, ny // 2 + 1):
                w_copy(j, step, way).wait_send()
        for step in range(NZ // 2):
            z_copy(step, way).wait_send()
        for i in range(NC):
            for step in range(ny // 2):
                y_copy(i, step, way).wait_send()
    for h in range(2):
        @pl.when(2 * core + h != k)
        def _():
            for array in range(2):
                sent(w_own.at[h, array], a_send.at[h, array])
    for j in range(NC - 1):
        w_sib(j).wait_send()
    for i in range(NC):
        grad_sib(i).wait_send()
        if order[2 * i][0] != 0:
            back_copy(i).wait_send()
        else:
            @pl.when(core != holder)
            def _():
                back_copy(i).wait_send()


def solution(mesh):
    n_row, n_depth = mesh.shape["row"], mesh.shape["depth"]

    def per_device(normed, up_weight, down_weight, out_grad):
        block, width = normed.shape
        hidden = up_weight.shape[1]
        m = block * n_row // 2
        share = hidden // 2
        slab = share // n_depth
        factor = 1.0 / math.sqrt(block * n_row * n_depth)
        dma = pltpu.SemaphoreType.DMA
        vmem = pltpu.VMEM
        whole = pl.BlockSpec(memory_space=pltpu.VMEM)
        y_half = n_depth // 2
        return pl.pallas_call(
            functools.partial(kernel, (block, m, share, slab, n_depth), factor),
            out_shape=(
                jax.ShapeDtypeStruct((block, width), BF16),
                jax.ShapeDtypeStruct((block, width), BF16),
                jax.ShapeDtypeStruct((width // n_depth, hidden), F32),
                jax.ShapeDtypeStruct((hidden // n_depth, width), F32),
            ),
            in_specs=[whole] * 4,
            out_specs=[whole] * 4,
            scratch_shapes=[
                vmem((2, NC, NX, 2, block, width), BF16),
                vmem((hidden, hidden), BF16),
                vmem((2, 2, slab, width), BF16),
                vmem((2, NC, n_depth, slab, width), BF16),
                vmem((NC, width, share), BF16),
                vmem((m, share), BF16),
                vmem((m, share), BF16),
                vmem((2, NC, n_depth, slab, width), BF16),
                vmem((NC, n_depth, slab, width), BF16),
                vmem((NC, y_half, 2, slab, width), BF16),
                vmem((NC, slab, width), BF16),
                vmem((2, 2, slab, width), BF16),
                vmem((NX, NC, 2, 2, block, width), BF16),
                vmem((8, 2, block, width), BF16),
                vmem((8, 2, 2, block, width), BF16),
                vmem((NZ, 2, block, width), BF16),
                vmem((NZ // 2, 2, 2, block, width), BF16),
                dma((NZ // 2, 2)), dma((NZ // 2, 2)),
                dma((8, 2, 2)), dma((8, 2, 2)),
                dma((2, 2)), dma((NC,)),
                dma((NC - 1, y_half, 2)), dma((NC - 1, y_half, 2)),
                dma((5,)), dma((5,)),
                dma((NC,)), dma((NC,)),
                dma((NC, y_half, 2)), dma((NC, y_half, 2)),
                dma((NC,)), dma((2, 2)),
                dma((8, 2, 2)), dma((8, 2, 2)),
                dma((NZ // 2, 2)), dma((NZ // 2, 2)),
            ],
            compiler_params=pltpu.CompilerParams(
                collective_id=0, has_side_effects=True, vmem_limit_bytes=56 * 1024 * 1024
            ),
            cost_estimate=pl.CostEstimate(flops=4_000_000_000, bytes_accessed=4_000_000, transcendentals=400_000),
        )(normed, up_weight, down_weight, out_grad)

    return jax.shard_map(
        per_device,
        mesh=mesh,
        in_specs=(P(("depth", "row"), "col"), P("col", "row"), P("row", "col"), P(("depth", "row"), "col")),
        out_specs=(
            P(("depth", "row"), "col"),
            P(("depth", "row"), "col"),
            P(("col", "depth"), "row"),
            P(("row", "depth"), "col"),
        ),
        check_vma=False,
    )
```

time: 383 us -> 117 us (0.31)
  waiting for transfers between devices: 301 us -> 0 us
  Pallas kernels: 0 us -> 109 us
  blocking collectives: 48.1 us -> 0 us
  matrix products: 15.1 us -> 0 us
  between operations: 13.8 us -> 0.64 us
  local copies, waits for them, and re-layouts: 1.78 us -> 6.23 us
    psum x2 -> x0, waiting for transfers between devices: 166 us -> none  [the longest x1 88.3 us: per_device(): lax.psum(up_part.astype(jnp.bfloat16), 'col').astype(jnp.float32)]
    reduce_scatter x2 -> x0, waiting for transfers between devices: 134 us -> none  [the longest x1 68.1 us: per_device(): lax.psum_scatter(input_part.astype(jnp.bfloat16), 'row', scatter_dimensio...]
    pallas_call x0 -> x1, Pallas kernels: none -> 109 us  [per_device(): pl.pallas_call(functools.partial(kernel, (block, m, share, slab, n_depth)...]
    all_gather x2 -> x0, blocking collectives: 48.1 us -> none  [the longest x1 27.8 us: per_device(): lax.all_gather(normed, 'row', axis=0, tiled=True)]
    dot_general x6 -> x0, matrix products: 15.1 us -> none  [the longest x2 6 us: contract_first(): lax.dot_general(left, right, (((0,), (0,)), ((), ())), preferred_element_...]
    unnamed x12 -> x4, local copies, waits for them, and re-layouts: 1.78 us -> 6.23 us
  transfers between devices with their start and end apart: 4 -> 0, of which waited for: 4 -> 0; matrix products, arithmetic and copies ran while one was open for 2% -> 0% of each run, Pallas kernels for 0% -> 0%
where the time goes in v2:
time: 117 us; the launch traced here: 116 us
  Pallas kernels  109 us (93%)
  local copies, waits for them, and re-layouts  6.23 us (5%)
    pallas_call x1, Pallas kernels, per_device(): pl.pallas_call(functools.partial(kernel, (block, m, share, slab, n_depth)...  109 us
    unnamed x4, local copies, waits for them, and re-layouts  6.23 us

profile of v2, /device:TPU:1, one launch (start us, length us, event | category | flops | bytes accessed | tf_op | source)
XLA Modules:
  0.0 116.3 jit_solution(3688793348541631014)
XLA Ops:
  0.6 109.5 %shard_map.75 = (bf16[32,768]{1,0:T(8,128)(2,1)}, bf16[32,768]{1,0:T(8,128)(2,1)}, f32[96,768]{1,0:T(8,128)}, f32[96,768]{1,0:T(8,128)}) custom-call(bf16[32,768]{1,0:T(8,128)(2,1)} %normed.1, bf16[768,768]{1,0:T(8,128)(2,1)} %up_weight.1, bf16[768,768]{1,0:T(8,128)(2,1)} %down_weight.1, bf16[32,768]{1,0:T(8,128)(2,1)} %out_grad.1), custom_call_target="tpu_custom_call" | custom-call | flops 4000000000 | bytes 4000000 | tf_op jit(solution)/shard_map/pallas_call | solution.py:449
  110.1 1.4 %copy.12 = bf16[32,768]{1,0:T(8,128)(2,1)} copy(bf16[32,768]{1,0:T(8,128)(2,1)} %get-tuple-element.8) | data formatting | bytes 98304
  111.5 1.4 %copy.13 = bf16[32,768]{1,0:T(8,128)(2,1)} copy(bf16[32,768]{1,0:T(8,128)(2,1)} %get-tuple-element.9) | data formatting | bytes 98304
  112.9 1.7 %copy.14 = f32[96,768]{1,0:T(8,128)} copy(f32[96,768]{1,0:T(8,128)} %get-tuple-element.10) | data formatting | bytes 589824
  114.6 1.7 %copy.15 = f32[96,768]{1,0:T(8,128)} copy(f32[96,768]{1,0:T(8,128)} %get-tuple-element.11) | data formatting | bytes 589824

commit v3 on v0

v3 whole, which is shorter than its diff:
```python
import functools
import math

import jax
import jax.numpy as jnp
from jax import lax
from jax.experimental import pallas as pl
from jax.experimental.pallas import tpu as pltpu
from jax.sharding import PartitionSpec as P

MESH = pl.DeviceIdType.MESH
BF16, F32 = jnp.bfloat16, jnp.float32
NX, NZ, NC = 4, 8, 4
PARTS = 3
ORDER = (
    ("nz", 1), ("prep",), ("own_out",), ("nz", 2), ("nx", 0, 1), ("cx", 0), ("own_in",), ("nx", 1, 1), ("nx", 2, 1),
    ("wy", 0, 1), ("nx", 0, 2), ("cx", 1), ("nx", 1, 2), ("wy", 1, 1), ("nx", 2, 2), ("wy", 0, 2), ("cx", 2),
    ("nz", 3), ("wy", 2, 1), ("cz", 0, 2), ("wy", 1, 2), ("cz", 1, 2), ("wy", 0, 3), ("cz", 2, 2), ("nx", 3, 1),
    ("cz", 3, 2), ("wy", 2, 2), ("nx", 4, 1), ("nz", 4), ("wy", 1, 3), ("cz", 0, 3), ("nx", 3, 2), ("cz", 1, 3),
    ("wy", 0, 4), ("nx", 4, 2), ("cz", 2, 3), ("nx", 5, 1), ("wy", 2, 3), ("cz", 3, 3), ("nz", 5), ("nx", 6, 1),
    ("wy", 1, 4), ("cz", 0, 4), ("wy", 0, 5), ("nx", 5, 2), ("cz", 1, 4), ("cz", 2, 4), ("wy", 2, 4), ("nx", 7, 1),
    ("w_in", 0), ("cz", 3, 4), ("wy", 1, 5), ("nx", 6, 2), ("cz", 0, 5), ("cz", 1, 5), ("cz", 2, 5), ("w_in", 1),
    ("wy", 2, 5), ("nx", 7, 2), ("cz", 3, 5), ("tok_in",), ("F", 0), ("wg", 0), ("w_in", 2), ("F", 2), ("wg", 2),
    ("gy", 0, 0), ("F", 1), ("wg", 1), ("gy", 2, 0), ("inputs",), ("gy", 0, 1), ("outputs",), ("gy", 1, 0),
    ("gy", 2, 1), ("bz", 0, 1), ("bz", 1, 1), ("bz", 2, 1), ("ox", 0, 1), ("bz", 3, 1), ("gy", 0, 2), ("ox", 1, 1),
    ("ox", 2, 1), ("gy", 1, 1), ("ox", 3, 1), ("ox", 4, 1), ("bz", 0, 2), ("ox", 5, 1), ("ox", 6, 1), ("bz", 1, 2),
    ("gy", 2, 2), ("ox", 7, 1), ("bz", 2, 2), ("ox", 0, 2), ("oz", 0), ("bz", 3, 2), ("gy", 0, 3), ("ox", 1, 2),
    ("bz", 0, 3), ("ox", 2, 2), ("bz", 1, 3), ("gy", 1, 2), ("ox", 3, 2), ("bz", 2, 3), ("ox", 4, 2), ("gy", 2, 3),
    ("ox", 5, 2), ("bz", 3, 3), ("oz", 1), ("ox", 6, 2), ("bz", 0, 4), ("gy", 0, 4), ("ox", 7, 2), ("bz", 1, 4),
    ("bz", 2, 4), ("gy", 1, 3), ("bx", 0), ("bz", 3, 4), ("oz", 2), ("gy", 2, 4), ("bx", 1), ("gy", 1, 4), ("oz", 3),
    ("oz", 4),
)


def dot(left, right):
    return jnp.dot(left, right, preferred_element_type=F32)


def contract_last(left, right):
    return lax.dot_general(left, right, (((1,), (1,)), ((), ())), preferred_element_type=F32)


def contract_first(left, right):
    return lax.dot_general(left, right, (((0,), (0,)), ((), ())), preferred_element_type=F32)


def gelu_parts(value):
    coeff = math.sqrt(2.0 / math.pi)
    square = value * value
    tangent = jnp.tanh(coeff * (value + 0.044715 * square * value))
    half = 0.5 * (1.0 + tangent)
    slope = half + 0.5 * value * (1.0 - tangent * tangent) * coeff * (1.0 + 3.0 * 0.044715 * square)
    return value * half, slope


def add(first, second):
    return (first.astype(F32) + second.astype(F32)).astype(BF16)


def wrap(index, by, size):
    return lax.rem(index + by + size, size)


def kernel(
    shape,
    normed, up_hbm, down_hbm, out_grad,
    token_sums, weight_sums,
    up_weight, down_weight, load,
    tokens, tokens_t, perm, w_own, weights, up_share,
    act, pre_grad, grads, grads_sib, grads_in, grads_own, grads_back,
    out, out_half, out_full, ring, ring_in, back, back_in, back_own, back_half, back_full,
    tz_send, tz_recv, tx_send, tx_recv, ux_send, ux_recv, uz_send, uz_recv,
    a_send, a_recv, w_send, w_recv, s_send, s_recv,
    g_send, g_recv, y_send, y_recv, b_send, b_recv,
    x_send, x_recv, z_send, z_recv, v_send, v_recv, c_send, c_recv,
):
    block, m, parts, slab, ny = shape
    width = normed.shape[1]
    hidden = up_weight.shape[1]
    w = slab * ny
    pieces = width // w
    share = parts * w
    lanes = width // 2
    row, k, depth = lax.axis_index("row"), lax.axis_index("col"), lax.axis_index("depth")
    x, zl, core = row // 4, lax.rem(row // 2, 2), lax.rem(row, 2)
    z = 2 * k + zl
    holder, half_of = k // 2, lax.rem(k, 2)

    def at(x_, z_, core_):
        return {"row": x_ * 4 + lax.rem(z_, 2) * 2 + core_, "col": z_ // 2}

    def peer(k_, core_):
        return {"row": x * 4 + zl * 2 + core_, "col": k_}

    x_right, x_left, x_far = wrap(x, 1, NX), wrap(x, -1, NX), wrap(x, 2, NX)
    to_x = (at(x_right, z, core), at(x_left, z, core))
    to_z = (at(x, wrap(z, 1, NZ), core), at(x, wrap(z, -1, NZ), core))
    to_y = ({"depth": wrap(depth, 1, ny)}, {"depth": wrap(depth, -1, ny)})
    to_sib = peer(k, 1 - core)

    def copy(src, dst, send, recv, to):
        return pltpu.make_async_remote_copy(
            src_ref=src, dst_ref=dst, send_sem=send, recv_sem=recv, device_id=to, device_id_type=MESH
        )

    def got(dst, recv):
        copy(dst, dst, recv, recv, to_sib).wait_recv()

    def sent(src, send):
        copy(src, src, send, send, to_sib).wait_send()

    def cut(way):
        return slice(way * lanes, (way + 1) * lanes)

    barrier = pltpu.get_barrier_semaphore()
    others = [peer(wrap(k, by, NC), core_) for by in (1, 2, 3) for core_ in (0, 1)]
    partners = (*to_x, *to_z, *to_y, to_sib, *others)
    for to in partners:
        pl.semaphore_signal(barrier, inc=1, device_id=to, device_id_type=MESH)
    loads = (pltpu.make_async_copy(up_hbm, up_weight, load.at[0]), pltpu.make_async_copy(down_hbm, down_weight, load.at[1]))
    for one in loads:
        one.start()
    tokens[0, k, x, zl] = normed[...]
    tokens[1, k, x, zl] = out_grad[...]
    pl.semaphore_wait(barrier, len(partners))

    def ref(array, x_, slot, way=None):
        if way is None:
            return tokens.at[array, slot // 2, x_, lax.rem(slot, 2)]
        return tokens.at[array, slot // 2, x_, lax.rem(slot, 2), :, cut(way)]

    def z_slot(step, way):
        return wrap(z, -(1 if way == 0 else -1) * step, NZ)

    def ring_copy(array, x_, step, way, send, recv):
        view = ref(array, x_, z_slot(step - 1, way), None if step < NZ // 2 else way)
        return copy(view, view, send.at[step - 1, way], recv.at[step - 1, way], to_z[way])

    def ring_got(array, x_, step, way, recv):
        got(ref(array, x_, z_slot(step, way), None if step < NZ // 2 else way), recv.at[step - 1, way])

    offsets = (0, -1, 1, -2, 2, -3, 3, 4)

    def tx_copy(n, step, way):
        slot = wrap(z, offsets[n], NZ)
        view = ref(0, x, slot) if step == 0 else ref(0, x_left if way == 0 else x_right, slot, way)
        return copy(view, view, tx_send.at[n, step, way], tx_recv.at[n, step, way], to_x[way])

    def normed_z(step):
        for way in range(2):
            if step > 1:
                ring_got(0, x, step - 1, way, tz_recv)
            if step <= NZ // 2:
                ring_copy(0, x, step, way, tz_send, tz_recv).start()
            if 1 < step <= NZ // 2:
                for way_x in range(2):
                    tx_copy(2 * (step - 1) - 1 + way, 0, way_x).start()
        if step == 1 or step == NZ // 2 + 1:
            for way_x in range(2):
                tx_copy(0 if step == 1 else 7, 0, way_x).start()

    def normed_x(n, step):
        slot = wrap(z, offsets[n], NZ)
        for way in range(2):
            if step == 1:
                got(ref(0, x_left if way == 0 else x_right, slot), tx_recv.at[n, 0, way])
                tx_copy(n, 1, way).start()
            else:
                got(ref(0, x_far, slot, way), tx_recv.at[n, 1, way])

    def ux_copy(step, way):
        view = ref(1, x, z) if step == 0 else ref(1, x_left if way == 0 else x_right, z, way)
        return copy(view, view, ux_send.at[step, way], ux_recv.at[step, way], to_x[way])

    streams = (x, x_left, x_right, x_far)

    def cotangent_x(step):
        for way in range(2):
            if step == 1:
                got(ref(1, x_left if way == 0 else x_right, z), ux_recv.at[0, way])
                ux_copy(1, way).start()
            elif step == 2:
                got(ref(1, x_far, z, way), ux_recv.at[1, way])
            else:
                ux_copy(0, way).start()
        for e in ((0,), (1, 2), (3,))[step]:
            cotangent_z(e, 1)

    def cotangent_z(e, step):
        for way in range(2):
            if step > 1:
                ring_got(1, streams[e], step - 1, way, uz_recv.at[e])
            if step <= NZ // 2:
                ring_copy(1, streams[e], step, way, uz_send.at[e], uz_recv.at[e]).start()

    rows = hidden // ny

    def pass_on(b):
        for h in range(2):
            @pl.when(2 * core + h != k)
            def _():
                for array in range(2):
                    pass_copy(array, b, h).start()

    def pass_copy(array, b, h):
        to = 2 * core + h
        there = lax.rem(k - to + NC - 1, NC)
        return copy(
            w_own.at[h, array, b], weights.at[array, b, depth, there],
            a_send.at[h, array, b], a_recv.at[b, there], peer(to, array),
        )

    def prepare():
        for one in loads:
            one.wait()
        for h in range(2):
            for b in range(parts):
                w_own[h, 1, b] = down_weight[pl.ds(pl.multiple_of(depth * rows + (h * parts + b) * slab, slab), slab), :]
        inner = lax.broadcasted_iota(jnp.int32, (hidden, w), 1)
        index = (inner // slab) * rows + lax.rem(inner, slab)
        index = lax.broadcasted_iota(jnp.int32, (hidden, w), 0) - index
        for g in range(2 * parts):
            perm[:, g * w : (g + 1) * w] = jnp.where(index == g * slab, 1.0, 0.0).astype(BF16)
        mixed = dot(up_weight[pl.ds(pl.multiple_of(depth * rows, rows), rows), :], perm[...]).astype(BF16)
        for h in range(2):
            for b in range(parts):
                g = h * parts + b
                for i in range(pieces):
                    w_own[h, 0, b, :, i * w : (i + 1) * w] = mixed[i * slab : (i + 1) * slab, g * w : (g + 1) * w]
        for b in range(parts):
            pass_on(b)

    def own_copies():
        return (
            copy(weights.at[1, :, :, NC - 1], weights.at[1, :, :, NC - 1], s_send.at[parts], s_recv.at[parts], to_sib),
            copy(up_share.at[:, NC - 1], up_share.at[:, NC - 1], s_send.at[parts + 1], s_recv.at[parts + 1], to_sib),
        )

    def own_out():
        @pl.when(core == holder)
        def _():
            for b in range(parts):
                for d in range(ny):
                    base = d * rows + half_of * (parts * slab) + b * slab
                    weights[1, b, d, NC - 1] = down_weight[pl.ds(pl.multiple_of(base, slab), slab), :]
            here = pl.ds(pl.multiple_of(half_of * share, share), share)
            up_own = dot(up_weight[...], perm[:, here]).astype(BF16)
            for b in range(parts):
                up_share[b, NC - 1] = up_own[:, b * w : (b + 1) * w]
            for one in own_copies():
                one.start()

    def own_in():
        @pl.when(core != holder)
        def _():
            got(weights.at[1, :, :, NC - 1], s_recv.at[parts])
            got(up_share.at[:, NC - 1], s_recv.at[parts + 1])

    def w_ref(b, step, way):
        slot = wrap(depth, -(1 if way == 0 else -1) * step, ny)
        if step < ny // 2:
            return weights.at[core, b, slot, 0 : NC - 1]
        return weights.at[core, b, slot, 0 : NC - 1, :, cut(way)]

    def w_copy(b, step, way):
        slot = wrap(depth, -(1 if way == 0 else -1) * (step - 1), ny)
        view = weights.at[core, b, slot, 0 : NC - 1]
        if step == ny // 2:
            view = weights.at[core, b, slot, 0 : NC - 1, :, cut(way)]
        return copy(view, view, w_send.at[b, step - 1, way], w_recv.at[b, step - 1, way], to_y[way])

    def w_sib(b):
        view = weights.at[core, b, :, 0 : NC - 1]
        return copy(view, view, s_send.at[b], s_recv.at[b], to_sib)

    def weights_y(b, step):
        if step == 1:
            for there in range(NC - 1):
                got(weights.at[core, b, depth, there], a_recv.at[b, there])
        for way in range(2):
            if step > 1:
                got(w_ref(b, step - 1, way), w_recv.at[b, step - 2, way])
            if step <= ny // 2:
                w_copy(b, step, way).start()
        if step == ny // 2 + 1:
            w_sib(b).start()

    def weights_in(b):
        got(weights.at[1 - core, b, :, 0 : NC - 1], s_recv.at[b])
        for there in range(NC - 1):
            for d in range(ny):
                for i in range(pieces):
                    base = (pieces * d + i) * slab
                    up_share[b, there, base : base + slab, :] = weights[0, b, d, there, :, i * w : (i + 1) * w]

    def feature(there):
        return wrap(k, 1 + there, NC)

    def tokens_in():
        for c in range(NC):
            tokens_t[c] = tokens[0, c].reshape(m, width).T

    def down_share(b, there):
        return weights[1, b, :, there].reshape(w, width)

    def forward(b):
        up = sum(dot(tokens[0, feature(i)].reshape(m, width), up_share[b, i]) for i in range(NC))
        cotangent = sum(contract_last(tokens[1, feature(i)].reshape(m, width), down_share(b, i)) for i in range(NC))
        active, slope = gelu_parts(up)
        act[b] = active.astype(BF16)
        pre_grad[b] = (cotangent * slope).astype(BF16)

    def grad_sib(b):
        return copy(grads.at[1 - core, b], grads_sib.at[b], g_send.at[b], g_recv.at[b], to_sib)

    def weight_grads(b):
        for i in range(NC):
            c = feature(i)
            down = contract_first(act[b], tokens[1, c].reshape(m, width)).astype(BF16)
            grads[1, b, :, i] = down.reshape(ny, slab, width)
            upper = dot(tokens_t[c], pre_grad[b]).astype(BF16)
            for d in range(ny):
                for j in range(pieces):
                    base = (pieces * d + j) * slab
                    grads[0, b, d, i, :, j * w : (j + 1) * w] = upper[base : base + slab, :]
        grad_sib(b).start()

    def y_copy(b, step, way):
        slot = wrap(depth, (1 if way == 0 else -1) * (ny // 2 - step), ny)
        src, dst = grads.at[core, b, slot], grads_in.at[b, step, way]
        if step == 0:
            some = slice(2 * way, 2 * way + 2)
            src, dst = grads.at[core, b, slot, some], grads_in.at[b, 0, way, some]
        return copy(src, dst, y_send.at[b, step, way], y_recv.at[b, step, way], to_y[way])

    def back_copy(b, there):
        return copy(
            grads_own.at[b, there], grads_back.at[core, half_of, b],
            b_send.at[b, there], b_recv.at[core, half_of, b], peer(feature(there), holder),
        )

    def grads_y(b, step):
        if step == 0:
            got(grads_sib.at[b], g_recv.at[b])
            grads[core, b] = add(grads[core, b], grads_sib[b])
        if step < ny // 2:
            for way in range(2):
                slot = wrap(depth, (1 if way == 0 else -1) * (ny // 2 - step), ny)
                some = slice(2 * way, 2 * way + 2)
                if step > 0:
                    y_copy(b, step - 1, way).wait_recv()
                if step == 1:
                    grads[core, b, slot, some] = add(grads[core, b, slot, some], grads_in[b, 0, way, some])
                elif step > 1:
                    grads[core, b, slot] = add(grads[core, b, slot], grads_in[b, step - 1, way])
                y_copy(b, step, way).start()
            return
        for way in range(2):
            y_copy(b, step - 1, way).wait_recv()
        total = grads[core, b, depth].astype(F32) + grads_in[b, step - 1, 0].astype(F32) + grads_in[b, step - 1, 1].astype(F32)
        grads_own[b] = total.astype(BF16)
        for there in range(NC - 1):
            back_copy(b, there).start()

        @pl.when(core == holder)
        def _():
            grads_back[core, half_of, b] = grads_own[b, NC - 1]

        @pl.when(core != holder)
        def _():
            back_copy(b, NC - 1).start()

    targets = (x_far, x_right, x_left, x)

    def back_ref(e, step, way):
        slot = wrap(z, (1 if way == 0 else -1) * (NZ // 2 - step), NZ)
        index = (targets[e], slot // 2, lax.rem(slot, 2))
        return (*index, slice(None), cut(way)) if step == 0 else index

    def back_z_copy(e, step, way):
        dst = (e, 0, way, slice(None), cut(way)) if step == 0 else (e, step, way)
        return copy(back.at[back_ref(e, step, way)], back_in.at[dst], v_send.at[e, step, way], v_recv.at[e, step, way], to_z[way])

    def back_x_copy(step, way):
        if step == 0:
            src, dst = back_own.at[0, :, cut(way)], back_half.at[way, :, cut(way)]
        else:
            src, dst = back_own.at[1 + way], back_full.at[way]
        return copy(src, dst, c_send.at[step, way], c_recv.at[step, way], to_x[way])

    def inputs():
        cotangent = jnp.concatenate([pre_grad[b] for b in range(parts)], axis=1)
        for i in range(NC):
            weight = jnp.concatenate([up_share[b, i] for b in range(parts)], axis=1)
            back[:, feature(i)] = contract_last(cotangent, weight).astype(BF16).reshape(NX, 2, block, width)
        for e in range(NX):
            for way in range(2):
                back_z_copy(e, 0, way).start()

    def back_z(e, step):
        if step < NZ // 2:
            for way in range(2):
                back_z_copy(e, step - 1, way).wait_recv()
                index = back_ref(e, step, way)
                if step == 1:
                    index = (*index, slice(None), cut(way))
                    back[index] = add(back[index], back_in[e, 0, way, :, cut(way)])
                else:
                    back[index] = add(back[index], back_in[e, step - 1, way])
                back_z_copy(e, step, way).start()
            return
        for way in range(2):
            back_z_copy(e, step - 1, way).wait_recv()
        total = back[targets[e], k, zl].astype(F32) + back_in[e, step - 1, 0].astype(F32) + back_in[e, step - 1, 1].astype(F32)
        back_own[e] = total.astype(BF16)
        if e == 0:
            for way in range(2):
                back_x_copy(0, way).start()

    def back_x(step):
        for way in range(2):
            back_x_copy(step, way).wait_recv()
            if step == 0:
                back_own[1 + way, :, cut(way)] = add(back_own[1 + way, :, cut(way)], back_half[way, :, cut(way)])
                back_x_copy(1, way).start()
        if step == 1:
            total = back_own[3].astype(F32) + back_full[0].astype(F32) + back_full[1].astype(F32)
            token_sums[1] = total.astype(BF16)

    order = tuple((dc, flip) for dc in (2, 1, 3, 0) for flip in (0, 1))

    def place(n):
        dc, flip = order[n]
        return wrap(k, dc, NC), (zl if flip == 0 else 1 - zl)

    def out_copy(n, step, way):
        c, zs = place(n)
        if step == 0:
            src, dst = out.at[x_far, c, zs, :, cut(way)], out_half.at[n, way, :, cut(way)]
        else:
            src, dst = out.at[x_right if way == 0 else x_left, c, zs], out_full.at[n, way]
        return copy(src, dst, x_send.at[n, step, way], x_recv.at[n, step, way], to_x[way])

    def outputs():
        active = jnp.concatenate([act[b] for b in range(parts)], axis=1)
        for i in range(NC):
            dc = order[2 * i][0]
            there = (dc - 1) % NC
            weight = jnp.concatenate([down_share(b, there) for b in range(parts)], axis=0)
            out[:, feature(there)] = dot(active, weight).astype(BF16).reshape(NX, 2, block, width)
            for n in (2 * i, 2 * i + 1):
                for way in range(2):
                    out_copy(n, 0, way).start()

    def out_x(n, step):
        c, zs = place(n)
        for way in range(2):
            out_copy(n, step - 1, way).wait_recv()
            if step == 1:
                to_ = x_right if way == 0 else x_left
                out[to_, c, zs, :, cut(way)] = add(out[to_, c, zs, :, cut(way)], out_half[n, way, :, cut(way)])
                out_copy(n, 1, way).start()
        if step == 2:
            total = out[x, c, zs].astype(F32) + out_full[n, 0].astype(F32) + out_full[n, 1].astype(F32)
            ring[2 * c + zs] = total.astype(BF16)

    def z_copy(step, way):
        slot = wrap(z, (1 if way == 0 else -1) * (NZ // 2 - step), NZ)
        src, dst = ring.at[slot], ring_in.at[step, way]
        if step == 0:
            src, dst = ring.at[slot, :, cut(way)], ring_in.at[0, way, :, cut(way)]
        return copy(src, dst, z_send.at[step, way], z_recv.at[step, way], to_z[way])

    def out_z(step):
        if step == NZ // 2:
            for way in range(2):
                z_copy(step - 1, way).wait_recv()
            total = ring[z].astype(F32) + ring_in[step - 1, 0].astype(F32) + ring_in[step - 1, 1].astype(F32)
            token_sums[0] = total.astype(BF16)
            return
        for way in range(2):
            slot = wrap(z, (1 if way == 0 else -1) * (NZ // 2 - step), NZ)
            if step > 0:
                z_copy(step - 1, way).wait_recv()
            if step == 1:
                ring[slot, :, cut(way)] = add(ring[slot, :, cut(way)], ring_in[0, way, :, cut(way)])
            elif step > 1:
                ring[slot] = add(ring[slot], ring_in[step - 1, way])
            z_copy(step, way).start()

    steps = dict(
        cx=cotangent_x, cz=cotangent_z, nz=normed_z, nx=normed_x, prep=prepare, own_out=own_out, own_in=own_in,
        wy=weights_y, w_in=weights_in, tok_in=tokens_in, F=forward, wg=weight_grads, gy=grads_y,
        inputs=inputs, outputs=outputs, bz=back_z, bx=back_x, ox=out_x, oz=out_z,
    )
    for name, *index in ORDER:
        steps[name](*index)

    for h in range(2):
        for array in range(2):
            local = jnp.logical_and(2 * core + h == k, core == array)

            @pl.when(jnp.logical_not(local))
            def _():
                for b in range(parts):
                    got(grads_back.at[array, h, b], b_recv.at[array, h, b])

    for h in range(2):
        for b in range(parts):
            base = (h * parts + b) * slab
            weight_sums[1, base : base + slab, :] = grads_back[1, h, b]
    columns = [
        jnp.concatenate([grads_back[0, h, b, :, i * w : (i + 1) * w] for i in range(pieces)], axis=0)
        for h in range(2) for b in range(parts)
    ]
    weight_sums[0] = contract_last(jnp.concatenate(columns, axis=1), perm[...]).astype(BF16)

    for way in range(2):
        for step in range(1, NZ // 2 + 1):
            ring_copy(0, x, step, way, tz_send, tz_recv).wait_send()
            for e in range(4):
                ring_copy(1, streams[e], step, way, uz_send.at[e], uz_recv.at[e]).wait_send()
                back_z_copy(e, step - 1, way).wait_send()
            z_copy(step - 1, way).wait_send()
        for step in range(2):
            for n in range(8):
                tx_copy(n, step, way).wait_send()
                out_copy(n, step, way).wait_send()
            ux_copy(step, way).wait_send()
            back_x_copy(step, way).wait_send()
        for b in range(parts):
            for step in range(1, ny // 2 + 1):
                w_copy(b, step, way).wait_send()
                y_copy(b, step - 1, way).wait_send()
    for h in range(2):
        @pl.when(2 * core + h != k)
        def _():
            for array in range(2):
                for b in range(parts):
                    pass_copy(array, b, h).wait_send()
    for b in range(parts):
        w_sib(b).wait_send()
        grad_sib(b).wait_send()
        for there in range(NC - 1):
            back_copy(b, there).wait_send()

        @pl.when(core != holder)
        def _():
            back_copy(b, NC - 1).wait_send()

    @pl.when(core == holder)
    def _():
        for one in own_copies():
            one.wait_send()


def solution(mesh):
    n_row, n_depth = mesh.shape["row"], mesh.shape["depth"]

    def per_device(normed, up_weight, down_weight, out_grad):
        block, width = normed.shape
        hidden = up_weight.shape[1]
        m = block * n_row // 2
        parts = PARTS
        slab = hidden // 2 // parts // n_depth
        w = slab * n_depth
        factor = 1.0 / math.sqrt(block * n_row * n_depth)
        dma = pltpu.SemaphoreType.DMA
        vmem = pltpu.VMEM
        whole = pl.BlockSpec(memory_space=pltpu.VMEM)
        y_half = n_depth // 2
        token_sums, weight_sums = pl.pallas_call(
            functools.partial(kernel, (block, m, parts, slab, n_depth)),
            out_shape=(
                jax.ShapeDtypeStruct((2, block, width), BF16),
                jax.ShapeDtypeStruct((2, hidden // n_depth, width), BF16),
            ),
            in_specs=[whole, pl.BlockSpec(memory_space=pl.ANY), pl.BlockSpec(memory_space=pl.ANY), whole],
            out_specs=[whole] * 2,
            scratch_shapes=[
                vmem((width, hidden), BF16),
                vmem((hidden, width), BF16),
                dma((2,)),
                vmem((2, NC, NX, 2, block, width), BF16),
                vmem((NC, width, m), BF16),
                vmem((hidden, hidden), BF16),
                vmem((2, 2, parts, slab, width), BF16),
                vmem((2, parts, n_depth, NC, slab, width), BF16),
                vmem((parts, NC, width, w), BF16),
                vmem((parts, m, w), BF16),
                vmem((parts, m, w), BF16),
                vmem((2, parts, n_depth, NC, slab, width), BF16),
                vmem((parts, n_depth, NC, slab, width), BF16),
                vmem((parts, y_half, 2, NC, slab, width), BF16),
                vmem((parts, NC, slab, width), BF16),
                vmem((2, 2, parts, slab, width), BF16),
                vmem((NX, NC, 2, block, width), BF16),
                vmem((8, 2, block, width), BF16),
                vmem((8, 2, block, width), BF16),
                vmem((NZ, block, width), BF16),
                vmem((NZ // 2, 2, block, width), BF16),
                vmem((NX, NC, 2, block, width), BF16),
                vmem((NX, NZ // 2, 2, block, width), BF16),
                vmem((NX, block, width), BF16),
                vmem((2, block, width), BF16),
                vmem((2, block, width), BF16),
                dma((NZ // 2, 2)), dma((NZ // 2, 2)),
                dma((8, 2, 2)), dma((8, 2, 2)),
                dma((2, 2)), dma((2, 2)),
                dma((NX, NZ // 2, 2)), dma((NX, NZ // 2, 2)),
                dma((2, 2, parts)), dma((parts, NC - 1)),
                dma((parts, y_half, 2)), dma((parts, y_half, 2)),
                dma((parts + 2,)), dma((parts + 2,)),
                dma((parts,)), dma((parts,)),
                dma((parts, y_half, 2)), dma((parts, y_half, 2)),
                dma((parts, NC)), dma((2, 2, parts)),
                dma((8, 2, 2)), dma((8, 2, 2)),
                dma((NZ // 2, 2)), dma((NZ // 2, 2)),
                dma((NX, NZ // 2, 2)), dma((NX, NZ // 2, 2)),
                dma((2, 2)), dma((2, 2)),
            ],
            compiler_params=pltpu.CompilerParams(
                collective_id=0, has_side_effects=True, vmem_limit_bytes=56 * 1024 * 1024
            ),
            cost_estimate=pl.CostEstimate(flops=4_000_000_000, bytes_accessed=4_000_000, transcendentals=400_000),
        )(normed, up_weight, down_weight, out_grad)
        up_grad, down_grad = weight_sums[0].astype(F32) * factor, weight_sums[1].astype(F32) * factor
        return token_sums[0], token_sums[1], up_grad, down_grad

    return jax.shard_map(
        per_device,
        mesh=mesh,
        in_specs=(P(("depth", "row"), "col"), P("col", "row"), P("row", "col"), P(("depth", "row"), "col")),
        out_specs=(
            P(("depth", "row"), "col"),
            P(("depth", "row"), "col"),
            P(("col", "depth"), "row"),
            P(("row", "depth"), "col"),
        ),
        check_vma=False,
    )
```

time: 383 us -> 97 us (0.25)
  waiting for transfers between devices: 301 us -> 0 us
  Pallas kernels: 0 us -> 92.8 us
  blocking collectives: 48.1 us -> 0 us
  matrix products: 15.1 us -> 0 us
  between operations: 13.8 us -> 0.64 us
    psum x2 -> x0, waiting for transfers between devices: 166 us -> none  [the longest x1 88.3 us: per_device(): lax.psum(up_part.astype(jnp.bfloat16), 'col').astype(jnp.float32)]
    reduce_scatter x2 -> x0, waiting for transfers between devices: 134 us -> none  [the longest x1 68.1 us: per_device(): lax.psum_scatter(input_part.astype(jnp.bfloat16), 'row', scatter_dimensio...]
    pallas_call x0 -> x1, Pallas kernels: none -> 92.8 us  [per_device(): pl.pallas_call(functools.partial(kernel, (block, m, parts, slab, n_depth)...]
    all_gather x2 -> x0, blocking collectives: 48.1 us -> none  [the longest x1 27.8 us: per_device(): lax.all_gather(normed, 'row', axis=0, tiled=True)]
    dot_general x6 -> x0, matrix products: 15.1 us -> none  [the longest x2 6 us: contract_first(): lax.dot_general(left, right, (((0,), (0,)), ((), ())), preferred_element_...]
  transfers between devices with their start and end apart: 4 -> 0, of which waited for: 4 -> 0; matrix products, arithmetic and copies ran while one was open for 2% -> 0% of each run, Pallas kernels for 0% -> 0%
where the time goes in v3:
time: 97 us; the launch traced here: 96.8 us
  Pallas kernels  92.8 us (96%)
  other arithmetic  1.83 us (2%)
  local copies, waits for them, and re-layouts  1.46 us (2%)
    pallas_call x1, Pallas kernels, per_device(): pl.pallas_call(functools.partial(kernel, (block, m, parts, slab, n_depth)...  92.8 us

profile of v3, /device:TPU:1, one launch (start us, length us, event | category | flops | bytes accessed | tf_op | source)
XLA Modules:
  0.0 96.8 jit_solution(7488990050381420966)
XLA Ops:
  0.6 92.8 %shard_map.75 = (bf16[2,32,768]{2,1,0:T(8,128)(2,1)}, bf16[2,96,768]{2,1,0:T(8,128)(2,1)}) custom-call(bf16[32,768]{1,0:T(8,128)(2,1)} %normed.1, bf16[768,768]{1,0:T(8,128)(2,1)} %up_hbm.1, bf16[768,768]{1,0:T(8,128)(2,1)} %down_hbm.1, bf16[32,768]{1,0:T(8,128)(2,1)} %out_grad.1), custom_call_target="tpu_custom_call" | custom-call | flops 4000000000 | bytes 4000000 | tf_op jit(solution)/shard_map/pallas_call | solution.py:572
  93.5 1.5 %slice_bitcast_fusion = (bf16[32,768]{1,0:T(8,128)(2,1)}, bf16[32,768]{1,0:T(8,128)(2,1)}) fusion(bf16[2,32,768]{2,1,0:T(8,128)(2,1)} %get-tuple-element.6), kind=kLoop, calls=%fused_computation.2 | loop fusion | bytes 196608 | tf_op jit(solution)/shard_map/squeeze | solution.py:628
  94.9 1.8 %multiply_bitcast_fusion = (f32[96,768]{1,0:T(8,128)}, f32[96,768]{1,0:T(8,128)}) fusion(bf16[2,96,768]{2,1,0:T(8,128)(2,1)} %get-tuple-element.7), kind=kLoop, calls=%fused_computation | loop fusion | flops 294912 | bytes 884736 | tf_op jit(solution)/shard_map/mul | solution.py:627

commit v4 on v3

--- a/solution.py
+++ b/solution.py
@@ -13,23 +13,26 @@
 NX, NZ, NC = 4, 8, 4
 PARTS = 3
 ORDER = (
-    ("nz", 1), ("prep",), ("own_out",), ("nz", 2), ("nx", 0, 1), ("cx", 0), ("own_in",), ("nx", 1, 1), ("nx", 2, 1),
-    ("wy", 0, 1), ("nx", 0, 2), ("cx", 1), ("nx", 1, 2), ("wy", 1, 1), ("nx", 2, 2), ("wy", 0, 2), ("cx", 2),
-    ("nz", 3), ("wy", 2, 1), ("cz", 0, 2), ("wy", 1, 2), ("cz", 1, 2), ("wy", 0, 3), ("cz", 2, 2), ("nx", 3, 1),
-    ("cz", 3, 2), ("wy", 2, 2), ("nx", 4, 1), ("nz", 4), ("wy", 1, 3), ("cz", 0, 3), ("nx", 3, 2), ("cz", 1, 3),
-    ("wy", 0, 4), ("nx", 4, 2), ("cz", 2, 3), ("nx", 5, 1), ("wy", 2, 3), ("cz", 3, 3), ("nz", 5), ("nx", 6, 1),
-    ("wy", 1, 4), ("cz", 0, 4), ("wy", 0, 5), ("nx", 5, 2), ("cz", 1, 4), ("cz", 2, 4), ("wy", 2, 4), ("nx", 7, 1),
-    ("w_in", 0), ("cz", 3, 4), ("wy", 1, 5), ("nx", 6, 2), ("cz", 0, 5), ("cz", 1, 5), ("cz", 2, 5), ("w_in", 1),
-    ("wy", 2, 5), ("nx", 7, 2), ("cz", 3, 5), ("tok_in",), ("F", 0), ("wg", 0), ("w_in", 2), ("F", 2), ("wg", 2),
-    ("gy", 0, 0), ("F", 1), ("wg", 1), ("gy", 2, 0), ("inputs",), ("gy", 0, 1), ("outputs",), ("gy", 1, 0),
-    ("gy", 2, 1), ("bz", 0, 1), ("bz", 1, 1), ("bz", 2, 1), ("ox", 0, 1), ("bz", 3, 1), ("gy", 0, 2), ("ox", 1, 1),
-    ("ox", 2, 1), ("gy", 1, 1), ("ox", 3, 1), ("ox", 4, 1), ("bz", 0, 2), ("ox", 5, 1), ("ox", 6, 1), ("bz", 1, 2),
-    ("gy", 2, 2), ("ox", 7, 1), ("bz", 2, 2), ("ox", 0, 2), ("oz", 0), ("bz", 3, 2), ("gy", 0, 3), ("ox", 1, 2),
-    ("bz", 0, 3), ("ox", 2, 2), ("bz", 1, 3), ("gy", 1, 2), ("ox", 3, 2), ("bz", 2, 3), ("ox", 4, 2), ("gy", 2, 3),
-    ("ox", 5, 2), ("bz", 3, 3), ("oz", 1), ("ox", 6, 2), ("bz", 0, 4), ("gy", 0, 4), ("ox", 7, 2), ("bz", 1, 4),
-    ("bz", 2, 4), ("gy", 1, 3), ("bx", 0), ("bz", 3, 4), ("oz", 2), ("gy", 2, 4), ("bx", 1), ("gy", 1, 4), ("oz", 3),
-    ("oz", 4),
+    ("nz", 1), ("cx", 0), ("prep",), ("own_out",), ("nz", 2), ("nx", 0, 1), ("cx", 1), ("cz", 0, 2), ("own_in",),
+    ("wy", 0, 1), ("nx", 1, 1), ("wy", 1, 1), ("nx", 2, 1), ("nx", 0, 2), ("cx", 2), ("wy", 2, 1), ("nx", 1, 2),
+    ("wy", 0, 2), ("nz", 3), ("cz", 1, 2), ("nx", 2, 2), ("cz", 2, 2), ("wy", 1, 2), ("cz", 0, 3), ("cz", 3, 2),
+    ("wy", 2, 2), ("nx", 3, 1), ("nz", 4), ("cz", 1, 3), ("wy", 0, 3), ("cz", 2, 3), ("nx", 4, 1), ("cz", 0, 4),
+    ("wy", 1, 3), ("cz", 3, 3), ("nx", 3, 2), ("nz", 5), ("wy", 2, 3), ("cz", 1, 4), ("nx", 5, 1), ("cz", 2, 4),
+    ("cz", 0, 5), ("wy", 0, 4), ("nx", 6, 1), ("cz", 3, 4), ("nx", 4, 2), ("wy", 1, 4), ("cz", 1, 5), ("cz", 2, 5),
+    ("nx", 7, 1), ("wy", 2, 4), ("nx", 5, 2), ("wy", 0, 5), ("cz", 3, 5), ("nx", 6, 2), ("wy", 1, 5), ("w_in", 0),
+    ("nx", 7, 2), ("tok_in",), ("wy", 2, 5), ("F", 0), ("wg", 0), ("w_in", 2), ("F", 2), ("wg", 2), ("gy", 0, 0, 1),
+    ("gy", 0, 0, 0), ("w_in", 1), ("F", 1), ("wg", 1), ("gy", 2, 0, 0), ("inputs",), ("gy", 0, 1, 0), ("gy", 0, 1, 1),
+    ("outputs",), ("gy", 1, 0, 0), ("gy", 1, 0, 1), ("gy", 2, 0, 1), ("gy", 2, 1, 0), ("bz", 0, 1), ("bz", 1, 1),
+    ("gy", 0, 2, 0), ("drain",), ("bz", 2, 1), ("ox", 0, 1), ("bz", 3, 1), ("gy", 0, 2, 1), ("ox", 1, 1),
+    ("gy", 1, 1, 0), ("ox", 2, 1), ("gy", 1, 1, 1), ("ox", 3, 1), ("gy", 2, 1, 1), ("ox", 4, 1), ("bz", 0, 2),
+    ("ox", 5, 1), ("gy", 2, 2, 0), ("ox", 6, 1), ("bz", 1, 2), ("ox", 7, 1), ("gy", 0, 3, 0), ("bz", 2, 2),
+    ("ox", 0, 2), ("oz", 0), ("gy", 0, 3, 1), ("bz", 3, 2), ("ox", 1, 2), ("gy", 1, 2, 0), ("bz", 0, 3), ("ox", 2, 2),
+    ("gy", 1, 2, 1), ("bz", 1, 3), ("ox", 3, 2), ("gy", 2, 2, 1), ("bz", 2, 3), ("ox", 4, 2), ("gy", 2, 3, 0),
+    ("ox", 5, 2), ("oz", 1), ("gy", 0, 4, 0), ("bz", 3, 3), ("ox", 6, 2), ("gy", 0, 4, 1), ("bz", 0, 4), ("ox", 7, 2),
+    ("gy", 1, 3, 0), ("bz", 1, 4), ("gy", 1, 3, 1), ("bz", 2, 4), ("gy", 2, 3, 1), ("oz", 2), ("bx", 0),
+    ("gy", 2, 4, 0), ("gy", 1, 4, 0), ("bz", 3, 4), ("gy", 1, 4, 1), ("gy", 2, 4, 1), ("bx", 1), ("oz", 3), ("oz", 4),
 )
+FIRST = 2
 
 
 def dot(left, right):
@@ -81,6 +84,7 @@
     pieces = width // w
     share = parts * w
     lanes = width // 2
+    first = FIRST * w
     row, k, depth = lax.axis_index("row"), lax.axis_index("col"), lax.axis_index("depth")
     x, zl, core = row // 4, lax.rem(row // 2, 2), lax.rem(row, 2)
     z = 2 * k + zl
@@ -110,6 +114,9 @@
         copy(src, src, send, send, to_sib).wait_send()
 
     def cut(way):
+        return slice(way * (block // 2), (way + 1) * (block // 2))
+
+    def lane_cut(way):
         return slice(way * lanes, (way + 1) * lanes)
 
     barrier = pltpu.get_barrier_semaphore()
@@ -124,63 +131,71 @@
     tokens[1, k, x, zl] = out_grad[...]
     pl.semaphore_wait(barrier, len(partners))
 
-    def ref(array, x_, slot, way=None):
-        if way is None:
-            return tokens.at[array, slot // 2, x_, lax.rem(slot, 2)]
-        return tokens.at[array, slot // 2, x_, lax.rem(slot, 2), :, cut(way)]
+    segments = ((0, slice(0, width)), (1, slice(0, first)), (1, slice(first, width)))
+
+    def ref(segment, x_, slot, way=None):
+        array, columns = segments[segment]
+        return tokens.at[array, slot // 2, x_, lax.rem(slot, 2), slice(0, block) if way is None else cut(way), columns]
 
     def z_slot(step, way):
         return wrap(z, -(1 if way == 0 else -1) * step, NZ)
 
-    def ring_copy(array, x_, step, way, send, recv):
-        view = ref(array, x_, z_slot(step - 1, way), None if step < NZ // 2 else way)
+    def ring_copy(segment, x_, step, way, send, recv):
+        view = ref(segment, x_, z_slot(step - 1, way), None if step < NZ // 2 else way)
         return copy(view, view, send.at[step - 1, way], recv.at[step - 1, way], to_z[way])
 
-    def ring_got(array, x_, step, way, recv):
-        got(ref(array, x_, z_slot(step, way), None if step < NZ // 2 else way), recv.at[step - 1, way])
+    def ring_got(segment, x_, step, way, recv):
+        got(ref(segment, x_, z_slot(step, way), None if step < NZ // 2 else way), recv.at[step - 1, way])
 
     offsets = (0, -1, 1, -2, 2, -3, 3, 4)
 
-    def tx_copy(n, step, way):
+    def tz_copy(g, step, way):
+        return ring_copy(g, x, step, way, tz_send.at[g], tz_recv.at[g])
+
+    def tx_copy(g, n, step, way):
         slot = wrap(z, offsets[n], NZ)
-        view = ref(0, x, slot) if step == 0 else ref(0, x_left if way == 0 else x_right, slot, way)
-        return copy(view, view, tx_send.at[n, step, way], tx_recv.at[n, step, way], to_x[way])
+        view = ref(g, x, slot) if step == 0 else ref(g, x_left if way == 0 else x_right, slot, way)
+        return copy(view, view, tx_send.at[g, n, step, way], tx_recv.at[g, n, step, way], to_x[way])
 
     def normed_z(step):
         for way in range(2):
-            if step > 1:
-                ring_got(0, x, step - 1, way, tz_recv)
-            if step <= NZ // 2:
-                ring_copy(0, x, step, way, tz_send, tz_recv).start()
+            for g in range(2):
+                if step > 1:
+                    ring_got(g, x, step - 1, way, tz_recv.at[g])
+                if step <= NZ // 2:
+                    tz_copy(g, step, way).start()
             if 1 < step <= NZ // 2:
                 for way_x in range(2):
-                    tx_copy(2 * (step - 1) - 1 + way, 0, way_x).start()
+                    for g in range(2):
+                        tx_copy(g, 2 * (step - 1) - 1 + way, 0, way_x).start()
         if step == 1 or step == NZ // 2 + 1:
             for way_x in range(2):
-                tx_copy(0 if step == 1 else 7, 0, way_x).start()
+                for g in range(2):
+                    tx_copy(g, 0 if step == 1 else 7, 0, way_x).start()
 
     def normed_x(n, step):
         slot = wrap(z, offsets[n], NZ)
         for way in range(2):
+            for g in range(2):
+                if step == 1:
+                    got(ref(g, x_left if way == 0 else x_right, slot), tx_recv.at[g, n, 0, way])
+                    tx_copy(g, n, 1, way).start()
+                else:
+                    got(ref(g, x_far, slot, way), tx_recv.at[g, n, 1, way])
+
+    def ux_copy(step, way):
+        view = ref(2, x, z) if step == 0 else ref(2, x_left if way == 0 else x_right, z, way)
+        return copy(view, view, ux_send.at[step, way], ux_recv.at[step, way], to_x[way])
+
+    streams = (x, x_left, x_right, x_far)
+
+    def cotangent_x(step):
+        for way in range(2):
             if step == 1:
-                got(ref(0, x_left if way == 0 else x_right, slot), tx_recv.at[n, 0, way])
-                tx_copy(n, 1, way).start()
-            else:
-                got(ref(0, x_far, slot, way), tx_recv.at[n, 1, way])
-
-    def ux_copy(step, way):
-        view = ref(1, x, z) if step == 0 else ref(1, x_left if way == 0 else x_right, z, way)
-        return copy(view, view, ux_send.at[step, way], ux_recv.at[step, way], to_x[way])
-
-    streams = (x, x_left, x_right, x_far)
-
-    def cotangent_x(step):
-        for way in range(2):
-            if step == 1:
-                got(ref(1, x_left if way == 0 else x_right, z), ux_recv.at[0, way])
+                got(ref(2, x_left if way == 0 else x_right, z), ux_recv.at[0, way])
                 ux_copy(1, way).start()
             elif step == 2:
-                got(ref(1, x_far, z, way), ux_recv.at[1, way])
+                got(ref(2, x_far, z, way), ux_recv.at[1, way])
             else:
                 ux_copy(0, way).start()
         for e in ((0,), (1, 2), (3,))[step]:
@@ -189,9 +204,9 @@
     def cotangent_z(e, step):
         for way in range(2):
             if step > 1:
-                ring_got(1, streams[e], step - 1, way, uz_recv.at[e])
+                ring_got(2, streams[e], step - 1, way, uz_recv.at[e])
             if step <= NZ // 2:
-                ring_copy(1, streams[e], step, way, uz_send.at[e], uz_recv.at[e]).start()
+                ring_copy(2, streams[e], step, way, uz_send.at[e], uz_recv.at[e]).start()
 
     rows = hidden // ny
 
@@ -260,13 +275,13 @@
         slot = wrap(depth, -(1 if way == 0 else -1) * step, ny)
         if step < ny // 2:
             return weights.at[core, b, slot, 0 : NC - 1]
-        return weights.at[core, b, slot, 0 : NC - 1, :, cut(way)]
+        return weights.at[core, b, slot, 0 : NC - 1, :, lane_cut(way)]
 
     def w_copy(b, step, way):
         slot = wrap(depth, -(1 if way == 0 else -1) * (step - 1), ny)
         view = weights.at[core, b, slot, 0 : NC - 1]
         if step == ny // 2:
-            view = weights.at[core, b, slot, 0 : NC - 1, :, cut(way)]
+            view = weights.at[core, b, slot, 0 : NC - 1, :, lane_cut(way)]
         return copy(view, view, w_send.at[b, step - 1, way], w_recv.at[b, step - 1, way], to_y[way])
 
     def w_sib(b):
@@ -310,8 +325,13 @@
         act[b] = active.astype(BF16)
         pre_grad[b] = (cotangent * slope).astype(BF16)
 
-    def grad_sib(b):
-        return copy(grads.at[1 - core, b], grads_sib.at[b], g_send.at[b], g_recv.at[b], to_sib)
+    def some(h):
+        return slice(2 * h, 2 * h + 2)
+
+    def grad_sib(b, h):
+        return copy(
+            grads.at[1 - core, b, :, some(h)], grads_sib.at[b, :, some(h)], g_send.at[b, h], g_recv.at[b, h], to_sib
+        )
 
     def weight_grads(b):
         for i in range(NC):
@@ -323,15 +343,16 @@
                 for j in range(pieces):
                     base = (pieces * d + j) * slab
                     grads[0, b, d, i, :, j * w : (j + 1) * w] = upper[base : base + slab, :]
-        grad_sib(b).start()
-
-    def y_copy(b, step, way):
+            if i % 2 == 1:
+                grad_sib(b, i // 2).start()
+
+    def y_copy(b, step, way, h):
         slot = wrap(depth, (1 if way == 0 else -1) * (ny // 2 - step), ny)
-        src, dst = grads.at[core, b, slot], grads_in.at[b, step, way]
-        if step == 0:
-            some = slice(2 * way, 2 * way + 2)
-            src, dst = grads.at[core, b, slot, some], grads_in.at[b, 0, way, some]
-        return copy(src, dst, y_send.at[b, step, way], y_recv.at[b, step, way], to_y[way])
+        these = some(h) if step > 0 else slice(2 * h + way, 2 * h + way + 1)
+        return copy(
+            grads.at[core, b, slot, these], grads_in.at[b, step, way, these],
+            y_send.at[b, step, way, h], y_recv.at[b, step, way, h], to_y[way],
+        )
 
     def back_copy(b, there):
         return copy(
@@ -339,51 +360,51 @@
             b_send.at[b, there], b_recv.at[core, half_of, b], peer(feature(there), holder),
         )
 
-    def grads_y(b, step):
+    def grads_y(b, step, h):
         if step == 0:
-            got(grads_sib.at[b], g_recv.at[b])
-            grads[core, b] = add(grads[core, b], grads_sib[b])
+            got(grads_sib.at[b, :, some(h)], g_recv.at[b, h])
+            grads[core, b, :, some(h)] = add(grads[core, b, :, some(h)], grads_sib[b, :, some(h)])
         if step < ny // 2:
             for way in range(2):
                 slot = wrap(depth, (1 if way == 0 else -1) * (ny // 2 - step), ny)
-                some = slice(2 * way, 2 * way + 2)
+                these = some(h) if step > 1 else slice(2 * h + way, 2 * h + way + 1)
                 if step > 0:
-                    y_copy(b, step - 1, way).wait_recv()
-                if step == 1:
-                    grads[core, b, slot, some] = add(grads[core, b, slot, some], grads_in[b, 0, way, some])
-                elif step > 1:
-                    grads[core, b, slot] = add(grads[core, b, slot], grads_in[b, step - 1, way])
-                y_copy(b, step, way).start()
+                    y_copy(b, step - 1, way, h).wait_recv()
+                    grads[core, b, slot, these] = add(grads[core, b, slot, these], grads_in[b, step - 1, way, these])
+                y_copy(b, step, way, h).start()
             return
         for way in range(2):
-            y_copy(b, step - 1, way).wait_recv()
-        total = grads[core, b, depth].astype(F32) + grads_in[b, step - 1, 0].astype(F32) + grads_in[b, step - 1, 1].astype(F32)
-        grads_own[b] = total.astype(BF16)
-        for there in range(NC - 1):
-            back_copy(b, there).start()
-
-        @pl.when(core == holder)
-        def _():
-            grads_back[core, half_of, b] = grads_own[b, NC - 1]
-
-        @pl.when(core != holder)
-        def _():
-            back_copy(b, NC - 1).start()
+            y_copy(b, step - 1, way, h).wait_recv()
+        these = some(h)
+        total = grads[core, b, depth, these].astype(F32) + grads_in[b, step - 1, 0, these].astype(F32) + grads_in[b, step - 1, 1, these].astype(F32)
+        grads_own[b, these] = total.astype(BF16)
+        for there in (2 * h, 2 * h + 1):
+            if there < NC - 1:
+                back_copy(b, there).start()
+                continue
+
+            @pl.when(core == holder)
+            def _():
+                grads_back[core, half_of, b] = grads_own[b, NC - 1]
+
+            @pl.when(core != holder)
+            def _():
+                back_copy(b, NC - 1).start()
 
     targets = (x_far, x_right, x_left, x)
 
     def back_ref(e, step, way):
         slot = wrap(z, (1 if way == 0 else -1) * (NZ // 2 - step), NZ)
-        index = (targets[e], slot // 2, lax.rem(slot, 2))
-        return (*index, slice(None), cut(way)) if step == 0 else index
+        return (targets[e], slot // 2, lax.rem(slot, 2), *((cut(way),) if step < 2 else ()))
 
     def back_z_copy(e, step, way):
-        dst = (e, 0, way, slice(None), cut(way)) if step == 0 else (e, step, way)
-        return copy(back.at[back_ref(e, step, way)], back_in.at[dst], v_send.at[e, step, way], v_recv.at[e, step, way], to_z[way])
+        slot = back_ref(e, step, way)
+        src, dst = slot[:3] if step else slot, (e, step, way, *((cut(way),) if step == 0 else ()))
+        return copy(back.at[src], back_in.at[dst], v_send.at[e, step, way], v_recv.at[e, step, way], to_z[way])
 
     def back_x_copy(step, way):
         if step == 0:
-            src, dst = back_own.at[0, :, cut(way)], back_half.at[way, :, cut(way)]
+            src, dst = back_own.at[0, cut(way)], back_half.at[way, cut(way)]
         else:
             src, dst = back_own.at[1 + way], back_full.at[way]
         return copy(src, dst, c_send.at[step, way], c_recv.at[step, way], to_x[way])
@@ -392,36 +413,32 @@
         cotangent = jnp.concatenate([pre_grad[b] for b in range(parts)], axis=1)
         for i in range(NC):
             weight = jnp.concatenate([up_share[b, i] for b in range(parts)], axis=1)
-            back[:, feature(i)] = contract_last(cotangent, weight).astype(BF16).reshape(NX, 2, block, width)
+            sums = contract_last(cotangent, weight).astype(BF16)
+            back[:, feature(i)] = sums.reshape(NX, 2, block, width)
         for e in range(NX):
             for way in range(2):
                 back_z_copy(e, 0, way).start()
 
     def back_z(e, step):
-        if step < NZ // 2:
-            for way in range(2):
-                back_z_copy(e, step - 1, way).wait_recv()
+        for way in range(2):
+            back_z_copy(e, step - 1, way).wait_recv()
+            if step < NZ // 2:
                 index = back_ref(e, step, way)
-                if step == 1:
-                    index = (*index, slice(None), cut(way))
-                    back[index] = add(back[index], back_in[e, 0, way, :, cut(way)])
-                else:
-                    back[index] = add(back[index], back_in[e, step - 1, way])
+                landed = back_in[e, step - 1, way, cut(way)] if step == 1 else back_in[e, step - 1, way]
+                back[index] = add(back[index], landed)
                 back_z_copy(e, step, way).start()
-            return
-        for way in range(2):
-            back_z_copy(e, step - 1, way).wait_recv()
-        total = back[targets[e], k, zl].astype(F32) + back_in[e, step - 1, 0].astype(F32) + back_in[e, step - 1, 1].astype(F32)
-        back_own[e] = total.astype(BF16)
-        if e == 0:
-            for way in range(2):
-                back_x_copy(0, way).start()
+        if step == NZ // 2:
+            total = back[targets[e], k, zl].astype(F32) + back_in[e, step - 1, 0].astype(F32) + back_in[e, step - 1, 1].astype(F32)
+            back_own[e] = total.astype(BF16)
+            if e == 0:
+                for way in range(2):
+                    back_x_copy(0, way).start()
 
     def back_x(step):
         for way in range(2):
             back_x_copy(step, way).wait_recv()
             if step == 0:
-                back_own[1 + way, :, cut(way)] = add(back_own[1 + way, :, cut(way)], back_half[way, :, cut(way)])
+                back_own[1 + way, cut(way)] = add(back_own[1 + way, cut(way)], back_half[way, cut(way)])
                 back_x_copy(1, way).start()
         if step == 1:
             total = back_own[3].astype(F32) + back_full[0].astype(F32) + back_full[1].astype(F32)
@@ -436,7 +453,7 @@
     def out_copy(n, step, way):
         c, zs = place(n)
         if step == 0:
-            src, dst = out.at[x_far, c, zs, :, cut(way)], out_half.at[n, way, :, cut(way)]
+            src, dst = out.at[x_far, c, zs, cut(way)], out_half.at[n, way]
         else:
             src, dst = out.at[x_right if way == 0 else x_left, c, zs], out_full.at[n, way]
         return copy(src, dst, x_send.at[n, step, way], x_recv.at[n, step, way], to_x[way])
@@ -458,7 +475,7 @@
             out_copy(n, step - 1, way).wait_recv()
             if step == 1:
                 to_ = x_right if way == 0 else x_left
-                out[to_, c, zs, :, cut(way)] = add(out[to_, c, zs, :, cut(way)], out_half[n, way, :, cut(way)])
+                out[to_, c, zs, cut(way)] = add(out[to_, c, zs, cut(way)], out_half[n, way])
                 out_copy(n, 1, way).start()
         if step == 2:
             total = out[x, c, zs].astype(F32) + out_full[n, 0].astype(F32) + out_full[n, 1].astype(F32)
@@ -468,33 +485,80 @@
         slot = wrap(z, (1 if way == 0 else -1) * (NZ // 2 - step), NZ)
         src, dst = ring.at[slot], ring_in.at[step, way]
         if step == 0:
-            src, dst = ring.at[slot, :, cut(way)], ring_in.at[0, way, :, cut(way)]
+            src, dst = ring.at[slot, cut(way)], ring_in.at[0, way, cut(way)]
         return copy(src, dst, z_send.at[step, way], z_recv.at[step, way], to_z[way])
 
     def out_z(step):
-        if step == NZ // 2:
-            for way in range(2):
-                z_copy(step - 1, way).wait_recv()
-            total = ring[z].astype(F32) + ring_in[step - 1, 0].astype(F32) + ring_in[step - 1, 1].astype(F32)
-            token_sums[0] = total.astype(BF16)
-            return
         for way in range(2):
             slot = wrap(z, (1 if way == 0 else -1) * (NZ // 2 - step), NZ)
             if step > 0:
                 z_copy(step - 1, way).wait_recv()
             if step == 1:
-                ring[slot, :, cut(way)] = add(ring[slot, :, cut(way)], ring_in[0, way, :, cut(way)])
-            elif step > 1:
+                ring[slot, cut(way)] = add(ring[slot, cut(way)], ring_in[0, way, cut(way)])
+            elif 1 < step < NZ // 2:
                 ring[slot] = add(ring[slot], ring_in[step - 1, way])
-            z_copy(step, way).start()
+            if step < NZ // 2:
+                z_copy(step, way).start()
+        if step == NZ // 2:
+            total = ring[z].astype(F32) + ring_in[step - 1, 0].astype(F32) + ring_in[step - 1, 1].astype(F32)
+            token_sums[0] = total.astype(BF16)
+
+    def drain_gathers():
+        for way in range(2):
+            for step in range(1, NZ // 2 + 1):
+                for e in range(4):
+                    ring_copy(2, streams[e], step, way, uz_send.at[e], uz_recv.at[e]).wait_send()
+                for g in range(2):
+                    tz_copy(g, step, way).wait_send()
+            for step in range(2):
+                for n in range(8):
+                    for g in range(2):
+                        tx_copy(g, n, step, way).wait_send()
+                ux_copy(step, way).wait_send()
+            for b in range(parts):
+                for step in range(1, ny // 2 + 1):
+                    w_copy(b, step, way).wait_send()
+        for h in range(2):
+            @pl.when(2 * core + h != k)
+            def _():
+                for array in range(2):
+                    for b in range(parts):
+                        pass_copy(array, b, h).wait_send()
+        for b in range(parts):
+            w_sib(b).wait_send()
+
+        @pl.when(core == holder)
+        def _():
+            for one in own_copies():
+                one.wait_send()
+
+    def drain_sums():
+        for way in range(2):
+            for step in range(NZ // 2):
+                for e in range(4):
+                    back_z_copy(e, step, way).wait_send()
+                z_copy(step, way).wait_send()
+            for step in range(2):
+                for n in range(8):
+                    out_copy(n, step, way).wait_send()
+                back_x_copy(step, way).wait_send()
+            for b in range(parts):
+                for step in range(ny // 2):
+                    for h in range(2):
+                        y_copy(b, step, way, h).wait_send()
+        for b in range(parts):
+            for h in range(2):
+                grad_sib(b, h).wait_send()
 
     steps = dict(
         cx=cotangent_x, cz=cotangent_z, nz=normed_z, nx=normed_x, prep=prepare, own_out=own_out, own_in=own_in,
         wy=weights_y, w_in=weights_in, tok_in=tokens_in, F=forward, wg=weight_grads, gy=grads_y,
-        inputs=inputs, outputs=outputs, bz=back_z, bx=back_x, ox=out_x, oz=out_z,
+        inputs=inputs, outputs=outputs, bz=back_z, bx=back_x, ox=out_x, oz=out_z, drain=drain_gathers,
     )
     for name, *index in ORDER:
         steps[name](*index)
+
+    drain_sums()
 
     for h in range(2):
         for array in range(2):
@@ -515,32 +579,7 @@
     ]
     weight_sums[0] = contract_last(jnp.concatenate(columns, axis=1), perm[...]).astype(BF16)
 
-    for way in range(2):
-        for step in range(1, NZ // 2 + 1):
-            ring_copy(0, x, step, way, tz_send, tz_recv).wait_send()
-            for e in range(4):
-                ring_copy(1, streams[e], step, way, uz_send.at[e], uz_recv.at[e]).wait_send()
-                back_z_copy(e, step - 1, way).wait_send()
-            z_copy(step - 1, way).wait_send()
-        for step in range(2):
-            for n in range(8):
-                tx_copy(n, step, way).wait_send()
-                out_copy(n, step, way).wait_send()
-            ux_copy(step, way).wait_send()
-            back_x_copy(step, way).wait_send()
-        for b in range(parts):
-            for step in range(1, ny // 2 + 1):
-                w_copy(b, step, way).wait_send()
-                y_copy(b, step - 1, way).wait_send()
-    for h in range(2):
-        @pl.when(2 * core + h != k)
-        def _():
-            for array in range(2):
-                for b in range(parts):
-                    pass_copy(array, b, h).wait_send()
     for b in range(parts):
-        w_sib(b).wait_send()
-        grad_sib(b).wait_send()
         for there in range(NC - 1):
             back_copy(b, there).wait_send()
 
@@ -548,10 +587,12 @@
         def _():
             back_copy(b, NC - 1).wait_send()
 
-    @pl.when(core == holder)
-    def _():
-        for one in own_copies():
-            one.wait_send()
+
+def finish(factor, token_sums, weight_sums, branch_out, normed_grad, up_grad, down_grad):
+    branch_out[...] = token_sums[0]
+    normed_grad[...] = token_sums[1]
+    up_grad[...] = weight_sums[0].astype(F32) * factor
+    down_grad[...] = weight_sums[1].astype(F32) * factor
 
 
 def solution(mesh):
@@ -595,7 +636,7 @@
                 vmem((parts, NC, slab, width), BF16),
                 vmem((2, 2, parts, slab, width), BF16),
                 vmem((NX, NC, 2, block, width), BF16),
-                vmem((8, 2, block, width), BF16),
+                vmem((8, 2, block // 2, width), BF16),
                 vmem((8, 2, block, width), BF16),
                 vmem((NZ, block, width), BF16),
                 vmem((NZ // 2, 2, block, width), BF16),
@@ -604,15 +645,15 @@
                 vmem((NX, block, width), BF16),
                 vmem((2, block, width), BF16),
                 vmem((2, block, width), BF16),
-                dma((NZ // 2, 2)), dma((NZ // 2, 2)),
-                dma((8, 2, 2)), dma((8, 2, 2)),
+                dma((2, NZ // 2, 2)), dma((2, NZ // 2, 2)),
+                dma((2, 8, 2, 2)), dma((2, 8, 2, 2)),
                 dma((2, 2)), dma((2, 2)),
                 dma((NX, NZ // 2, 2)), dma((NX, NZ // 2, 2)),
                 dma((2, 2, parts)), dma((parts, NC - 1)),
                 dma((parts, y_half, 2)), dma((parts, y_half, 2)),
                 dma((parts + 2,)), dma((parts + 2,)),
-                dma((parts,)), dma((parts,)),
-                dma((parts, y_half, 2)), dma((parts, y_half, 2)),
+                dma((parts, 2)), dma((parts, 2)),
+                dma((parts, y_half, 2, 2)), dma((parts, y_half, 2, 2)),
                 dma((parts, NC)), dma((2, 2, parts)),
                 dma((8, 2, 2)), dma((8, 2, 2)),
                 dma((NZ // 2, 2)), dma((NZ // 2, 2)),
@@ -624,8 +665,15 @@
             ),
             cost_estimate=pl.CostEstimate(flops=4_000_000_000, bytes_accessed=4_000_000, transcendentals=400_000),
         )(normed, up_weight, down_weight, out_grad)
-        up_grad, down_grad = weight_sums[0].astype(F32) * factor, weight_sums[1].astype(F32) * factor
-        return token_sums[0], token_sums[1], up_grad, down_grad
+        return pl.pallas_call(
+            functools.partial(finish, factor),
+            out_shape=(
+                jax.ShapeDtypeStruct((block, width), BF16),
+                jax.ShapeDtypeStruct((block, width), BF16),
+                jax.ShapeDtypeStruct((width // n_depth, hidden), F32),
+                jax.ShapeDtypeStruct((hidden // n_depth, width), F32),
+            ),
+        )(token_sums, weight_sums)
 
     return jax.shard_map(
         per_device,

time: 97 us -> 92.5 us (0.954)
  other arithmetic: 1.83 us -> 0 us
  local copies, waits for them, and re-layouts: 1.46 us -> 0 us
  Pallas kernels: 92.8 us -> 91.7 us
    pallas_call x1, Pallas kernels: 92.8 us -> 89.8 us  [per_device(): pl.pallas_call(functools.partial(kernel, (block, m, parts, slab, n_depth)...]
    pallas_call x0 -> x1, Pallas kernels: none -> 1.87 us  [per_device(): pl.pallas_call(functools.partial(finish, factor), out_shape=(jax.ShapeDty...]
    mul x1 -> x0, other arithmetic: 1.83 us -> none  [per_device(): weight_sums[1].astype(F32) * factor]
    squeeze x1 -> x0, local copies, waits for them, and re-layouts: 1.46 us -> none  [per_device(): return (token_sums[0], token_sums[1], up_grad, down_grad)]
where the time goes in v4:
time: 92.5 us; the launch traced here: 92.3 us
  Pallas kernels  91.7 us (99%)
    pallas_call x1, Pallas kernels, per_device(): pl.pallas_call(functools.partial(kernel, (block, m, parts, slab, n_depth)...  89.8 us
    pallas_call x1, Pallas kernels, per_device(): pl.pallas_call(functools.partial(finish, factor), out_shape=(jax.ShapeDty...  1.87 us

profile of v4, /device:TPU:1, one launch (start us, length us, event | category | flops | bytes accessed | tf_op | source)
XLA Modules:
  0.0 92.3 jit_solution(3689172396611485534)
XLA Ops:
  0.6 89.8 %shard_map.75 = (bf16[2,32,768]{2,1,0:T(8,128)(2,1)}, bf16[2,96,768]{2,1,0:T(8,128)(2,1)}) custom-call(bf16[32,768]{1,0:T(8,128)(2,1)} %normed.1, bf16[768,768]{1,0:T(8,128)(2,1)} %up_hbm.1, bf16[768,768]{1,0:T(8,128)(2,1)} %down_hbm.1, bf16[32,768]{1,0:T(8,128)(2,1)} %out_grad.1), custom_call_target="tpu_custom_call" | custom-call | flops 4000000000 | bytes 4000000 | tf_op jit(solution)/shard_map/pallas_call | solution.py:613
  90.5 1.9 %shard_map.76 = (bf16[32,768]{1,0:T(8,128)(2,1)}, bf16[32,768]{1,0:T(8,128)(2,1)}, f32[96,768]{1,0:T(8,128)}, f32[96,768]{1,0:T(8,128)}) custom-call(bf16[2,32,768]{2,1,0:T(8,128)(2,1)} %get-tuple-element.6.token_sums, bf16[2,96,768]{2,1,0:T(8,128)(2,1)} %get-tuple-element.7.weight_sums), custom_call_target="tpu_custom_call" | custom-call | tf_op jit(solution)/shard_map/pallas_call | solution.py:668

commit v5 on v4

--- a/solution.py
+++ b/solution.py
@@ -66,7 +66,7 @@
 
 def kernel(
     shape,
-    normed, up_hbm, down_hbm, out_grad,
+    normed_hbm, up_hbm, down_hbm, out_grad_hbm,
     token_sums, weight_sums,
     up_weight, down_weight, load,
     tokens, tokens_t, perm, w_own, weights, up_share,
@@ -78,7 +78,7 @@
     x_send, x_recv, z_send, z_recv, v_send, v_recv, c_send, c_recv,
 ):
     block, m, parts, slab, ny = shape
-    width = normed.shape[1]
+    width = normed_hbm.shape[1]
     hidden = up_weight.shape[1]
     w = slab * ny
     pieces = width // w
@@ -124,11 +124,15 @@
     partners = (*to_x, *to_z, *to_y, to_sib, *others)
     for to in partners:
         pl.semaphore_signal(barrier, inc=1, device_id=to, device_id_type=MESH)
+    own = (
+        pltpu.make_async_copy(normed_hbm, tokens.at[0, k, x, zl], load.at[2]),
+        pltpu.make_async_copy(out_grad_hbm, tokens.at[1, k, x, zl], load.at[3]),
+    )
     loads = (pltpu.make_async_copy(up_hbm, up_weight, load.at[0]), pltpu.make_async_copy(down_hbm, down_weight, load.at[1]))
-    for one in loads:
+    for one in (*own, *loads):
         one.start()
-    tokens[0, k, x, zl] = normed[...]
-    tokens[1, k, x, zl] = out_grad[...]
+    for one in own:
+        one.wait()
     pl.semaphore_wait(barrier, len(partners))
 
     segments = ((0, slice(0, width)), (1, slice(0, first)), (1, slice(first, width)))
@@ -234,15 +238,15 @@
         inner = lax.broadcasted_iota(jnp.int32, (hidden, w), 1)
         index = (inner // slab) * rows + lax.rem(inner, slab)
         index = lax.broadcasted_iota(jnp.int32, (hidden, w), 0) - index
-        for g in range(2 * parts):
-            perm[:, g * w : (g + 1) * w] = jnp.where(index == g * slab, 1.0, 0.0).astype(BF16)
-        mixed = dot(up_weight[pl.ds(pl.multiple_of(depth * rows, rows), rows), :], perm[...]).astype(BF16)
-        for h in range(2):
-            for b in range(parts):
+        mine = up_weight[pl.ds(pl.multiple_of(depth * rows, rows), rows), :]
+        for b in range(parts):
+            picks = [jnp.where(index == (h * parts + b) * slab, 1.0, 0.0).astype(BF16) for h in range(2)]
+            mixed = dot(mine, jnp.concatenate(picks, axis=1)).astype(BF16)
+            for h in range(2):
                 g = h * parts + b
+                perm[:, g * w : (g + 1) * w] = picks[h]
                 for i in range(pieces):
-                    w_own[h, 0, b, :, i * w : (i + 1) * w] = mixed[i * slab : (i + 1) * slab, g * w : (g + 1) * w]
-        for b in range(parts):
+                    w_own[h, 0, b, :, i * w : (i + 1) * w] = mixed[i * slab : (i + 1) * slab, h * w : (h + 1) * w]
             pass_on(b)
 
     def own_copies():
@@ -588,7 +592,15 @@
             back_copy(b, NC - 1).wait_send()
 
 
-def finish(factor, token_sums, weight_sums, branch_out, normed_grad, up_grad, down_grad):
+def finish(factor, token_any, weight_any, branch_out, normed_grad, up_grad, down_grad, token_sums, weight_sums, load):
+    loads = (
+        pltpu.make_async_copy(token_any, token_sums, load.at[0]),
+        pltpu.make_async_copy(weight_any, weight_sums, load.at[1]),
+    )
+    for one in loads:
+        one.start()
+    for one in loads:
+        one.wait()
     branch_out[...] = token_sums[0]
     normed_grad[...] = token_sums[1]
     up_grad[...] = weight_sums[0].astype(F32) * factor
@@ -613,15 +625,15 @@
         token_sums, weight_sums = pl.pallas_call(
             functools.partial(kernel, (block, m, parts, slab, n_depth)),
             out_shape=(
-                jax.ShapeDtypeStruct((2, block, width), BF16),
-                jax.ShapeDtypeStruct((2, hidden // n_depth, width), BF16),
+                pltpu.VMEM((2, block, width), BF16),
+                pltpu.VMEM((2, hidden // n_depth, width), BF16),
             ),
-            in_specs=[whole, pl.BlockSpec(memory_space=pl.ANY), pl.BlockSpec(memory_space=pl.ANY), whole],
+            in_specs=[pl.BlockSpec(memory_space=pl.ANY)] * 4,
             out_specs=[whole] * 2,
             scratch_shapes=[
                 vmem((width, hidden), BF16),
                 vmem((hidden, width), BF16),
-                dma((2,)),
+                dma((4,)),
                 vmem((2, NC, NX, 2, block, width), BF16),
                 vmem((NC, width, m), BF16),
                 vmem((hidden, hidden), BF16),
@@ -673,6 +685,12 @@
                 jax.ShapeDtypeStruct((width // n_depth, hidden), F32),
                 jax.ShapeDtypeStruct((hidden // n_depth, width), F32),
             ),
+            in_specs=[pl.BlockSpec(memory_space=pl.ANY)] * 2,
+            scratch_shapes=[
+                vmem((2, block, width), BF16),
+                vmem((2, hidden // n_depth, width), BF16),
+                dma((2,)),
+            ],
         )(token_sums, weight_sums)
 
     return jax.shard_map(

time: 92.5 us -> 92.4 us (level)
  Pallas kernels: 91.7 us -> 90.2 us
  local copies, waits for them, and re-layouts: 0 us -> 1.34 us
    pallas_call x1, Pallas kernels: 89.8 us -> 88.4 us  [per_device(): pl.pallas_call(functools.partial(kernel, (block, m, parts, slab, n_depth)...]
    unnamed x0 -> x4, local copies, waits for them, and re-layouts: none -> 1.34 us
where the time goes in v5:
time: 92.4 us; the launch traced here: 92.2 us
  Pallas kernels  90.2 us (98%)
  local copies, waits for them, and re-layouts  1.34 us (1%)
    pallas_call x1, Pallas kernels, per_device(): pl.pallas_call(functools.partial(kernel, (block, m, parts, slab, n_depth)...  88.4 us
    pallas_call x1, Pallas kernels, per_device(): pl.pallas_call(functools.partial(finish, factor), out_shape=(jax.ShapeDty...  1.88 us

profile of v5, /device:TPU:1, one launch (start us, length us, event | category | flops | bytes accessed | tf_op | source)
XLA Modules:
  0.0 92.2 jit_solution(744458885888306661)
XLA Ops:
  0.6 88.4 %shard_map.75 = (bf16[2,32,768]{2,1,0:T(8,128)(2,1)S(1)}, bf16[2,96,768]{2,1,0:T(8,128)(2,1)S(1)}) custom-call(bf16[32,768]{1,0:T(8,128)(2,1)} %normed_hbm.1, bf16[768,768]{1,0:T(8,128)(2,1)} %up_hbm.1, bf16[768,768]{1,0:T(8,128)(2,1)} %down_hbm.1, bf16[32,768]{1,0:T(8,128)(2,1)} %out_grad_hbm.1), custom_call_target="tpu_custom_call" | custom-call | flops 4000000000 | bytes 4000000 | tf_op jit(solution)/shard_map/pallas_call | solution.py:625
  89.0 0.0 copy-start
  89.0 0.7 copy-done
  89.7 0.0 copy-start.1
  89.7 0.6 copy-done.1
  90.3 1.9 %shard_map.76 = (bf16[32,768]{1,0:T(8,128)(2,1)}, bf16[32,768]{1,0:T(8,128)(2,1)}, f32[96,768]{1,0:T(8,128)}, f32[96,768]{1,0:T(8,128)}) custom-call(bf16[2,32,768]{2,1,0:T(8,128)(2,1)} %copy-done.1, bf16[2,96,768]{2,1,0:T(8,128)(2,1)} %copy-done), custom_call_target="tpu_custom_call" | custom-call | tf_op jit(solution)/shard_map/pallas_call | solution.py:680
Async XLA Ops:
  89.0 0.7 copy-start
  89.7 0.6 copy-start.1
